TPU v7x, 128 devices: a whole 4x4x4 slice. The times are simulated.
128 devices in a mesh: cam: 32 (over y, x, core), row: 4 (over z).
Axes of the slice: x: 4, y: 4, z: 4, core: 2. Of those that a mesh axis runs over, the one named last changes fastest.
Arguments:
- image: bfloat16 [32, 16, 128, 2048], P('cam', None, 'row'), may hold values from -6 to 6
- conv_first: bfloat16 [16, 144], replicated, may hold values from -0.5 to 0.5
- conv_second: bfloat16 [16, 144], replicated, may hold values from -0.5 to 0.5
- conv_uv: bfloat16 [16, 144], replicated, may hold values from -0.5 to 0.5
- send_block: int32 [32, 4, 128, 16], P('cam', 'row'), may hold values from 0 to 511
- send_shift: int32 [32, 4, 128, 16], P('cam', 'row'), may hold values from 0 to 127
- send_weight: int32 [32, 4, 128, 16], P('cam', 'row'), may hold values from 1 to 64
- send_count: int32 [32, 4, 128], P('cam', 'row'), may hold values from 0 to 16, as said below
- recv_tile: int32 [4, 32, 128, 16], P('row', 'cam'), may hold values from 0 to 1023
Outputs:
- texture: bfloat16 [16, 4096, 4096], P(None, 'row', 'cam')
Inputs may be any that keep to these rules, and one draw needn't show every extreme that they name: `send_count`: slots of a list at or beyond its count are padding. In every draw one atlas region receives 16 used slots from every strip.
All inputs are finite; a program needn't handle non-finite values.
Results may differ from a plain program's by a relative error of at most 0.0066.
Values may be sent and summed in bfloat16 or wider, within the bound.
A program may use at most 192 MiB of HBM per device.

v0:
```python
import math

import jax
import jax.numpy as jnp
from jax import lax
from jax.sharding import PartitionSpec as P

TL = 128
AR_DEV = 1024


def with_halo(cells, sides, width):
    for axis, dim in sides:
        count = lax.axis_size(axis)
        ends = count - 1
        head = lax.slice_in_dim(cells, 0, width, axis=dim)
        tail = lax.slice_in_dim(cells, cells.shape[dim] - width, cells.shape[dim], axis=dim)
        cells = jnp.concatenate(
            [
                lax.ppermute(tail, axis, [(i, (i + 1) % count) for i in range(ends)]),
                cells,
                lax.ppermute(head, axis, [((i + 1) % count, i) for i in range(ends)]),
            ],
            axis=dim,
        )
    return cells


def conv_taps(padded, weight):
    channels = padded.shape[0]
    height = padded.shape[1] - 2
    width = padded.shape[2] - 2
    total = jnp.zeros((weight.shape[0], height, width), jnp.float32)
    for row_step in range(3):
        for col_step in range(3):
            offset = (row_step * 3 + col_step) * channels
            kernel = weight[:, offset : offset + channels]
            window = padded[:, row_step : row_step + height, col_step : col_step + width]
            total = total + jnp.einsum(
                "oi,ihw->ohw", kernel, window, preferred_element_type=jnp.float32
            )
    return total


def pad_columns(field):
    return jnp.pad(field, ((0, 0), (0, 0), (1, 1)))


def local(
    image,
    conv_first,
    conv_second,
    conv_uv,
    send_block,
    send_shift,
    send_weight,
    send_count,
    recv_tile,
):
    pixels = image[0]
    channels, strip_rows, width = pixels.shape
    deeper = with_halo(pixels, (("row", 1),), 2)
    hidden = jax.nn.silu(conv_taps(pad_columns(deeper), conv_first))
    global_row = (
        lax.axis_index("row") * strip_rows
        - 1
        + lax.broadcasted_iota(jnp.int32, (1, strip_rows + 2, 1), 1)
    )
    inside = (global_row >= 0) & (global_row < strip_rows * lax.axis_size("row"))
    hidden = jnp.where(inside, hidden, 0.0).astype(jnp.bfloat16)
    features = conv_taps(pad_columns(hidden), conv_second).astype(jnp.bfloat16)
    tile_len = TL
    per_row = width // tile_len
    blocks = (
        features.reshape(channels, strip_rows, per_row, tile_len)
        .transpose(1, 2, 0, 3)
        .reshape(strip_rows * per_row, channels, tile_len)
    )
    peers = send_block.shape[2]
    capacity = send_block.shape[3]
    entries = peers * capacity
    picked = jnp.take(blocks, send_block.reshape(entries), axis=0)
    shifts = send_shift.reshape(entries)
    group = math.gcd(entries, 128)
    source_pos = lax.broadcasted_iota(jnp.int32, (1, tile_len, tile_len), 1)
    target_pos = lax.broadcasted_iota(jnp.int32, (1, tile_len, tile_len), 2)

    def shift_blocks(operands):
        block_group, offsets = operands
        table = (source_pos == (target_pos - offsets[:, None, None]) % tile_len).astype(
            jnp.bfloat16
        )
        return jnp.einsum("eck,ekj->ecj", block_group, table, preferred_element_type=jnp.float32)

    shifted = lax.map(
        shift_blocks,
        (
            picked.reshape(entries // group, group, channels, tile_len),
            shifts.reshape(entries // group, group),
        ),
    )
    slot_pos = lax.broadcasted_iota(jnp.int32, (peers, capacity), 1)
    valid = slot_pos < send_count.reshape(peers, 1)
    scales = jnp.where(valid, send_weight.reshape(peers, capacity).astype(jnp.float32) / 16.0, 0.0)
    payload = (
        shifted.reshape(peers, capacity, channels, tile_len) * scales[:, :, None, None]
    ).astype(jnp.bfloat16)
    scale_wire = scales.astype(jnp.bfloat16)
    arrived, arrived_scale = (
        lax.all_to_all(payload, ("cam", "row"), split_axis=0, concat_axis=0, tiled=True),
        lax.all_to_all(scale_wire, ("cam", "row"), split_axis=0, concat_axis=0, tiled=True),
    )
    incoming = arrived.reshape(entries, channels * tile_len)
    tile_ids = recv_tile.reshape(entries)
    onehot = (lax.broadcasted_iota(jnp.int32, (AR_DEV, entries), 0) == tile_ids[None, :]).astype(
        jnp.bfloat16
    )
    gathered = jnp.dot(onehot, incoming, preferred_element_type=jnp.float32)
    weight_sum = jnp.dot(
        onehot, arrived_scale.reshape(entries, 1), preferred_element_type=jnp.float32
    )
    joined = (gathered / jnp.maximum(weight_sum, 1.0)).astype(jnp.bfloat16)
    atlas = joined.reshape(AR_DEV, channels, tile_len).transpose(1, 0, 2)
    rimmed = with_halo(atlas, (("cam", 2), ("row", 1)), 1)
    blended = atlas.astype(jnp.float32) + conv_taps(rimmed, conv_uv)
    return blended.astype(jnp.bfloat16)


def solution(mesh):
    return jax.shard_map(
        local,
        mesh=mesh,
        in_specs=(
            P("cam", None, "row", None),
            P(),
            P(),
            P(),
            P("cam", "row", None, None),
            P("cam", "row", None, None),
            P("cam", "row", None, None),
            P("cam", "row", None),
            P("row", "cam", None, None),
        ),
        out_specs=P(None, "row", "cam"),
        check_vma=False,
    )
```

profile of v0, /device:TPU:47, one launch (start us, length us, event | category | flops | bytes accessed | tf_op | source)
XLA Modules:
  0.0 436.8 jit_solution(1563180625647007010)
XLA Ops:
  2.3 10.9 %all-to-all-start.1 = ((bf16[128,1,16]{2,1,0:T(2,128)(2,1)}), bf16[128,1,16]{2,1,0:T(2,128)(2,1)}, u32[]{:S(2)}, u32[]{:S(2)}) async-start(bf16[128,1,16]{2,1,0:T(2,128)(2,1)} %fusion.114), calls=%async_computation.1 | async-start | bytes 131072 | tf_op jit(solution)/shard_map/all_to_all | solution.py:111
  16.0 3.4 collective-permute-start
  22.7 3.0 collective-permute-done.1
  29.7 3.0 fusion.72
  41.2 2.9 fusion.60
  47.0 11.6 %fusion.34 = bf16[16,34,2048]{2,0,1:T(8,128)(2,1)S(1)} fusion(f32[34,2048,16]{1,2,0:T(8,128)} %fusion.64, f32[34,2048,16]{1,2,0:T(8,128)} %fusion.70, f32[34,2048,16]{1,2,0:T(8,128)} %fusion.72, f32[34,2048,16]{1,2,0:T(8,128)} %fusion.58, f32[34,2048,16]{1,2,0:T(8,128)} %fusion.74, f32[34,2048,16]{1,2,0:T(8,128)S(1)} %fusion.76, ...), kind=kOutput, calls=%fused_computation.43 | convolution fusion | flops 51249152 | bytes 40243712 | tf_op jit(solution)/shard_map/oi,ihw->ohw/dot_general | solution.py:39
  76.7 9.3 %fusion.97 = bf16[32,2,16,8,128]{4,3,2,1,0:T(8,128)(2,1)S(1)} fusion(f32[32,2048,16]{1,2,0:T(8,128)} %fusion.80, f32[32,2048,16]{1,2,0:T(8,128)} %fusion.87, f32[32,2048,16]{1,2,0:T(8,128)} %fusion.89, f32[32,2048,16]{1,2,0:T(8,128)} %fusion.82, f32[32,2048,16]{1,2,0:T(8,128)S(1)} %fusion.91, f32[32,2048,16]{1,2,0:T(8,128)S(1)} %fusion.93, ...), kind=kOutput, calls=%fused_computation.108 | convolution fusion | flops 42991616 | bytes 37883904 | tf_op jit(solution)/shard_map/oi,ihw->ohw/dot_general | solution.py:39
  86.4 16.3 %gather_fusion = bf16[2048,16,128]{2,1,0:T(8,128)(2,1)} fusion(bf16[512,16,128]{2,1,0:T(8,128)(2,1)S(1)} %bitcast.166, s32[2048]{0:T(1024)S(1)} %broadcast_clamp_fusion), kind=kCustom, calls=%fused_computation | custom fusion | bytes 16785408 | tf_op jit(solution)/shard_map/jit(_take)/gather | solution.py:82
  102.7 8.1 %broadcast_select_fusion = bf16[16,128,16,128]{3,2,1,0:T(8,128)(2,1)} fusion(bf16[16,128,16,128]{3,2,1,0:T(8,128)(2,1)} %bitcast.171, pred[16,128]{1,0:T(8,128)(4,1)S(1)} %compare_and_fusion), kind=kLoop, calls=%fused_computation.36 | loop fusion | flops 4194304 | bytes 16779264 | tf_op jit(solution)/shard_map/jit(_take)/select_n | solution.py:82
  110.8 58.7 %while.15 = (s32[]{:T(128)}, f32[16,128,16,128]{3,2,1,0:T(8,128)}, bf16[16,128,16,128]{3,2,1,0:T(8,128)(2,1)}, s32[16,128]{1,0:T(8,128)S(1)}, s32[]{:T(128)}) while((s32[]{:T(128)}, f32[16,128,16,128]{3,2,1,0:T(8,128)}, bf16[16,128,16,128]{3,2,1,0:T(8,128)(2,1)}, s32[16,128]{1,0:T(8,128)S(1)}, s32[]{:T(128)}) %tuple.39), condition=%wide.region_1.2_spmd.clone.clone, body=%wide.region_0.1_spmd.clone.clone.sunk | while | flops 94371840 | bytes 1575497 | solution.py:95
  110.8 3.7 fusion.197
  114.5 3.6 fusion.197
  118.1 3.7 fusion.197
  121.8 3.6 fusion.197
  125.4 3.7 fusion.197
  129.1 3.6 fusion.197
  132.8 3.6 fusion.197
  136.4 3.7 fusion.197
  140.1 3.7 fusion.197
  143.8 3.7 fusion.197
  147.5 3.6 fusion.197
  151.2 3.7 fusion.197
  154.8 3.7 fusion.197
  158.5 3.7 fusion.197
  162.2 3.7 fusion.197
  165.9 3.6 fusion.197
  169.5 9.7 %multiply_convert_fusion = bf16[128,16,16,128]{3,2,1,0:T(8,128)(2,1)} fusion(f32[128,16,16,128]{3,2,1,0:T(8,128)} %bitcast.172, f32[128,16]{1,0:T(8,128)S(1)} %bitcast_select_fusion), kind=kLoop, calls=%fused_computation.25 | loop fusion | flops 8388608 | bytes 25174016 | tf_op jit(solution)/shard_map/convert_element_type | solution.py:107
  179.2 11.1 %all-to-all-start = ((bf16[128,16,16,128]{3,2,1,0:T(8,128)(2,1)}), bf16[128,16,16,128]{3,2,1,0:T(8,128)(2,1)}, u32[]{:S(2)}, u32[]{:S(2)}) async-start(bf16[128,16,16,128]{3,2,1,0:T(8,128)(2,1)} %multiply_convert_fusion), calls=%async_computation | async-start | bytes 16777216 | tf_op jit(solution)/shard_map/all_to_all | solution.py:110
  193.1 100.7 %all-to-all-done = bf16[128,16,16,128]{3,2,1,0:T(8,128)(2,1)} async-done(((bf16[128,16,16,128]{3,2,1,0:T(8,128)(2,1)}), bf16[128,16,16,128]{3,2,1,0:T(8,128)(2,1)}, u32[]{:S(2)}, u32[]{:S(2)}) %all-to-all-start) | async-done | bytes 8388640 | tf_op jit(solution)/shard_map/all_to_all | solution.py:110
  293.7 11.3 %fusion.53 = bf16[128,8,16,128]{3,1,2,0:T(8,128)(2,1)S(1)} fusion(f32[1024]{0:T(1024)S(1)} %broadcast_maximum_fusion, bf16[256,8,16,128]{3,2,1,0:T(8,128)(2,1)} %bitcast.52, s32[2048]{0:T(1024)S(1)} %eq.22), kind=kOutput, calls=%fused_computation.65 | convolution fusion | flops 8596226048 | bytes 12595200 | tf_op jit(solution)/shard_map/dot_general | solution.py:118
  306.5 4.6 %fusion.187 = (bf16[16,1024,1]{2,0,1:T(8,128)(2,1)}, bf16[16,1024,1]{2,0,1:T(8,128)(2,1)}) fusion(bf16[16,1024,128]{2,0,1:T(8,128)(2,1)S(1)} %bitcast.159), kind=kLoop, calls=%fused_computation.207 | loop fusion | bytes 131072 | tf_op jit(solution)/shard_map/slice | solution.py:17
  311.1 4.8 %copy.30 = bf16[16,1024,1]{1,0,2:T(8,128)(2,1)S(1)} copy(bf16[16,1024,1]{2,0,1:T(8,128)(2,1)} %get-tuple-element.127) | data formatting | bytes 65536 | tf_op jit(solution)/shard_map/slice | solution.py:17
  315.9 4.8 %copy.31 = bf16[16,1024,1]{1,0,2:T(8,128)(2,1)S(1)} copy(bf16[16,1024,1]{2,0,1:T(8,128)(2,1)} %get-tuple-element.128) | data formatting | bytes 65536 | tf_op jit(solution)/shard_map/slice | solution.py:16
  322.6 6.2 %collective-permute-start.2 = (bf16[16,1024,1]{1,0,2:T(8,128)(2,1)S(1)}, bf16[16,1024,1]{1,0,2:T(8,128)(2,1)S(1)}, u32[]{:S(2)}, u32[]{:S(2)}) collective-permute-start(bf16[16,1024,1]{1,0,2:T(8,128)(2,1)S(1)} %copy.30), channel_id=1, source_target_pairs={{0,4},{4,8},{8,12},{12,16},{16,20},{20,24},{24,28},{28,32},{32,36}... | collective-permute-start | bytes 98312 | tf_op jit(solution)/shard_map/ppermute | solution.py:20
  328.8 6.7 %fusion.119 = f32[1024,128,16]{1,2,0:T(8,128)} fusion(bf16[16,144]{1,0:T(8,128)(2,1)S(1)} %copy-done.5, bf16[1024,16,128]{2,1,0:T(8,128)(2,1)} %bitcast.160), kind=kOutput, calls=%fused_computation.137 | convolution fusion | flops 67108864 | bytes 12587008 | tf_op jit(solution)/shard_map/oi,ihw->ohw/dot_general | solution.py:39
  335.5 4.8 %copy.33 = bf16[16,1024,1]{2,0,1:T(8,128)(2,1)} copy(bf16[16,1024,1]{1,0,2:T(8,128)(2,1)S(1)} %collective-permute-done.3) | data formatting | bytes 65536 | tf_op jit(solution)/shard_map/ppermute | solution.py:22
  340.3 9.5 %fusion.41 = f32[1024,128,16]{1,2,0:T(8,128)} fusion(bf16[16,1024,1]{2,0,1:T(8,128)(2,1)} %copy.33, bf16[16,1024,128]{2,0,1:T(8,128)(2,1)} %bitcast.161, bf16[16,144]{1,0:T(8,128)(2,1)S(1)} %copy-done.5), kind=kOutput, calls=%fused_computation.51 | convolution fusion | flops 75497472 | bytes 12619776 | tf_op jit(solution)/shard_map/oi,ihw->ohw/dot_general | solution.py:39
  349.8 4.8 %copy.32 = bf16[16,1024,1]{2,0,1:T(8,128)(2,1)} copy(bf16[16,1024,1]{1,0,2:T(8,128)(2,1)S(1)} %collective-permute-done.2) | data formatting | bytes 65536 | tf_op jit(solution)/shard_map/ppermute | solution.py:20
  355.5 3.4 collective-permute-start.4
  361.4 5.3 %fusion.43 = f32[1024,128,16]{1,2,0:T(8,128)} fusion(bf16[16,1024,128]{2,0,1:T(8,128)(2,1)S(1)} %bitcast.164, bf16[16,1024,1]{2,0,1:T(8,128)(2,1)S(1)} %copy-done.3, bf16[16,144]{1,0:T(8,128)(2,1)S(1)} %copy-done.5), kind=kOutput, calls=%fused_computation.54 | convolution fusion | flops 75497472 | bytes 16781312 | tf_op jit(solution)/shard_map/oi,ihw->ohw/dot_general | solution.py:39
  366.7 13.3 %maximum_maximum_fusion = (bf16[16,1025,130]{2,0,1:T(8,128)(2,1)S(1)}, bf16[16,1025,130]{2,0,1:T(8,128)(2,1)S(1)}) fusion(bf16[16,1024,1]{2,0,1:T(8,128)(2,1)S(1)} %copy-done.2, bf16[16,1024,128]{2,0,1:T(8,128)(2,1)S(1)} %bitcast.165, bf16[16,1024,1]{2,0,1:T(8,128)(2,1)S(1)} %copy-done.3, bf16[16,1,130]{2,0,1:T(8,128)(2,1)S(1)} %collective-permute-done.4, ...), kind=kLoop, calls=%fused_computation.26 | loop fusion | flops 34112000 | bytes 12796160 | tf_op jit(solution)/shard_map/concatenate | solution.py:18
  380.0 5.2 %fusion.45 = f32[1024,128,16]{1,2,0:T(8,128)} fusion(bf16[16,1025,130]{2,0,1:T(8,128)(2,1)S(1)} %get-tuple-element.123, bf16[16,144]{1,0:T(8,128)(2,1)S(1)} %copy-done.5), kind=kOutput, calls=%fused_computation.56 | convolution fusion | flops 67108864 | bytes 12587008 | tf_op jit(solution)/shard_map/oi,ihw->ohw/dot_general | solution.py:39
  385.2 4.8 %fusion.47 = f32[1024,128,16]{1,2,0:T(8,128)} fusion(bf16[16,1025,130]{2,0,1:T(8,128)(2,1)S(1)} %get-tuple-element.123, bf16[16,144]{1,0:T(8,128)(2,1)S(1)} %copy-done.5), kind=kOutput, calls=%fused_computation.58 | convolution fusion | flops 67108864 | bytes 12587008 | tf_op jit(solution)/shard_map/oi,ihw->ohw/dot_general | solution.py:39
  390.0 4.4 %fusion.49 = f32[1024,128,16]{1,2,0:T(8,128)} fusion(bf16[16,1025,130]{2,0,1:T(8,128)(2,1)S(1)} %get-tuple-element.123, bf16[16,144]{1,0:T(8,128)(2,1)S(1)} %copy-done.5), kind=kOutput, calls=%fused_computation.60 | convolution fusion | flops 67108864 | bytes 12587008 | tf_op jit(solution)/shard_map/oi,ihw->ohw/dot_general | solution.py:39
  394.5 4.8 %fusion.37 = f32[1024,128,16]{1,2,0:T(8,128)} fusion(bf16[16,1025,130]{2,0,1:T(8,128)(2,1)S(1)} %get-tuple-element.124, bf16[16,144]{1,0:T(8,128)(2,1)S(1)} %copy-done.5), kind=kOutput, calls=%fused_computation.46 | convolution fusion | flops 67108864 | bytes 12587008 | tf_op jit(solution)/shard_map/oi,ihw->ohw/dot_general | solution.py:39
  399.3 4.5 %fusion.39 = f32[1024,128,16]{1,2,0:T(8,128)} fusion(bf16[16,1025,130]{2,0,1:T(8,128)(2,1)S(1)} %get-tuple-element.124, bf16[16,144]{1,0:T(8,128)(2,1)S(1)} %copy-done.5), kind=kOutput, calls=%fused_computation.48 | convolution fusion | flops 67108864 | bytes 12587008 | tf_op jit(solution)/shard_map/oi,ihw->ohw/dot_general | solution.py:39
  403.8 27.6 %fusion.28 = bf16[16,1024,128]{2,0,1:T(8,128)(2,1)} fusion(f32[1024,128,16]{1,2,0:T(8,128)} %fusion.37, f32[1024,128,16]{1,2,0:T(8,128)} %fusion.39, f32[1024,128,16]{1,2,0:T(8,128)} %fusion.41, f32[1024,128,16]{1,2,0:T(8,128)} %fusion.119, f32[1024,128,16]{1,2,0:T(8,128)} %fusion.43, f32[1024,128,16]{1,2,0:T(8,128)} %fusion.45, ...), kind=kOutput, calls=%fused_computation.32 | convolution fusion | flops 90177536 | bytes 79695872 | tf_op jit(solution)/shard_map/oi,ihw->ohw/dot_general | solution.py:39
  431.4 5.3 %copy.36 = bf16[16,1024,128]{2,1,0:T(8,128)(2,1)} copy(bf16[16,1024,128]{2,0,1:T(8,128)(2,1)} %fusion.28) | data formatting | bytes 8388608 | tf_op jit(solution)/shard_map/convert_element_type | solution.py:126
  (90 shorter events, 51.7 us)
Async XLA Ops:
  0.0 21.6 %copy-start.11 = (s32[1,1,128]{2,1,0:T(1,128)S(1)}, s32[1,1,128]{2,1,0:T(1,128)}, u32[]{:S(2)}) copy-start(s32[1,1,128]{2,1,0:T(1,128)} %param.18) | copy-start | bytes 1540
  0.0 21.3 %copy-start.8 = (s32[1,1,128,16]{2,3,1,0:T(8,128)S(1)}, s32[1,1,128,16]{2,3,1,0:T(8,128)}, u32[]{:S(2)}) copy-start(s32[1,1,128,16]{2,3,1,0:T(8,128)} %param.15) | copy-start | bytes 24580
  0.0 21.8 %copy-start.9 = (s32[1,1,128,16]{2,3,1,0:T(8,128)S(1)}, s32[1,1,128,16]{2,3,1,0:T(8,128)}, u32[]{:S(2)}) copy-start(s32[1,1,128,16]{2,3,1,0:T(8,128)} %param.16) | copy-start | bytes 24580
  2.3 176.9 %all-to-all-start.1 = ((bf16[128,1,16]{2,1,0:T(2,128)(2,1)}), bf16[128,1,16]{2,1,0:T(2,128)(2,1)}, u32[]{:S(2)}, u32[]{:S(2)}) async-start(bf16[128,1,16]{2,1,0:T(2,128)(2,1)} %fusion.114), calls=%async_computation.1 | async-start | bytes 131072 | tf_op jit(solution)/shard_map/all_to_all | solution.py:111
  13.3 12.8 %copy-start.6 = (bf16[16,144]{1,0:T(8,128)(2,1)S(1)}, bf16[16,144]{1,0:T(8,128)(2,1)}, u32[]{:S(2)}) copy-start(bf16[16,144]{1,0:T(8,128)(2,1)} %param.12) | copy-start | bytes 13828
  16.0 6.6 %collective-permute-start = (bf16[16,2,2048]{2,0,1:T(8,128)(2,1)S(1)}, bf16[16,2,2048]{2,0,1:T(8,128)(2,1)S(1)}, u32[]{:S(2)}, u32[]{:S(2)}) collective-permute-start(bf16[16,2,2048]{2,0,1:T(8,128)(2,1)S(1)} %get-tuple-element.129), channel_id=1, source_target_pairs={{0,1},{1,2},{2,3},{4,5},{5,6},{6,7},{8,9},{9,10},{10,11},{12,13},{... | collective-permute-start | bytes 393224 | tf_op jit(solution)/shard_map/ppermute | solution.py:20
  19.4 6.3 %collective-permute-start.1 = (bf16[16,2,2048]{2,0,1:T(8,128)(2,1)S(1)}, bf16[16,2,2048]{2,0,1:T(8,128)(2,1)S(1)}, u32[]{:S(2)}, u32[]{:S(2)}) collective-permute-start(bf16[16,2,2048]{2,0,1:T(8,128)(2,1)S(1)} %get-tuple-element.130), channel_id=1, source_target_pairs={{1,0},{2,1},{3,2},{5,4},{6,5},{7,6},{9,8},{10,9},{11,10},{13,12},{... | collective-permute-start | bytes 393224 | tf_op jit(solution)/shard_map/ppermute | solution.py:22
  47.0 11.6 %copy-start.7 = (bf16[16,144]{1,0:T(8,128)(2,1)S(1)}, bf16[16,144]{1,0:T(8,128)(2,1)}, u32[]{:S(2)}) copy-start(bf16[16,144]{1,0:T(8,128)(2,1)} %param.13) | copy-start | bytes 13828
  179.2 11.1 %copy-start.10 = (s32[1,1,128,16]{2,3,1,0:T(8,128)S(1)}, s32[1,1,128,16]{2,3,1,0:T(8,128)}, u32[]{:S(2)}) copy-start(s32[1,1,128,16]{2,3,1,0:T(8,128)} %param.19) | copy-start | bytes 24580
  179.2 114.6 %all-to-all-start = ((bf16[128,16,16,128]{3,2,1,0:T(8,128)(2,1)}), bf16[128,16,16,128]{3,2,1,0:T(8,128)(2,1)}, u32[]{:S(2)}, u32[]{:S(2)}) async-start(bf16[128,16,16,128]{3,2,1,0:T(8,128)(2,1)} %multiply_convert_fusion), calls=%async_computation | async-start | bytes 16777216 | tf_op jit(solution)/shard_map/all_to_all | solution.py:110
  306.5 4.6 %copy-start = (bf16[128,8,16,128]{3,2,1,0:T(8,128)(2,1)}, bf16[128,8,16,128]{3,2,1,0:T(8,128)(2,1)S(1)}, u32[]{:S(2)}) copy-start(bf16[128,8,16,128]{3,2,1,0:T(8,128)(2,1)S(1)} %copy.39) | copy-start | bytes 12582916
  311.1 17.7 %copy-start.5 = (bf16[16,144]{1,0:T(8,128)(2,1)S(1)}, bf16[16,144]{1,0:T(8,128)(2,1)}, u32[]{:S(2)}) copy-start(bf16[16,144]{1,0:T(8,128)(2,1)} %param.14) | copy-start | bytes 13828
  320.7 14.9 %collective-permute-start.3 = (bf16[16,1024,1]{1,0,2:T(8,128)(2,1)S(1)}, bf16[16,1024,1]{1,0,2:T(8,128)(2,1)S(1)}, u32[]{:S(2)}, u32[]{:S(2)}) collective-permute-start(bf16[16,1024,1]{1,0,2:T(8,128)(2,1)S(1)} %copy.31), channel_id=1, source_target_pairs={{4,0},{8,4},{12,8},{16,12},{20,16},{24,20},{28,24},{32,28},{36,32}... | collective-permute-start | bytes 98312 | tf_op jit(solution)/shard_map/ppermute | solution.py:22
  322.6 27.2 %collective-permute-start.2 = (bf16[16,1024,1]{1,0,2:T(8,128)(2,1)S(1)}, bf16[16,1024,1]{1,0,2:T(8,128)(2,1)S(1)}, u32[]{:S(2)}, u32[]{:S(2)}) collective-permute-start(bf16[16,1024,1]{1,0,2:T(8,128)(2,1)S(1)} %copy.30), channel_id=1, source_target_pairs={{0,4},{4,8},{8,12},{12,16},{16,20},{20,24},{24,28},{28,32},{32,36}... | collective-permute-start | bytes 98312 | tf_op jit(solution)/shard_map/ppermute | solution.py:20
  354.6 6.8 %copy-start.1 = (bf16[128,8,16,128]{3,2,1,0:T(8,128)(2,1)S(1)}, bf16[128,8,16,128]{3,2,1,0:T(8,128)(2,1)}, u32[]{:S(2)}) copy-start(bf16[128,8,16,128]{3,2,1,0:T(8,128)(2,1)} %copy-done) | copy-start | bytes 12582916
  354.6 6.8 %copy-start.3 = (bf16[16,1024,1]{2,0,1:T(8,128)(2,1)S(1)}, bf16[16,1024,1]{2,0,1:T(8,128)(2,1)}, u32[]{:S(2)}) copy-start(bf16[16,1024,1]{2,0,1:T(8,128)(2,1)} %copy.32) | copy-start | bytes 98308
  355.5 11.1 %collective-permute-start.4 = (bf16[16,1,130]{2,0,1:T(8,128)(2,1)S(1)}, bf16[16,1,130]{2,0,1:T(8,128)(2,1)S(1)}, u32[]{:S(2)}, u32[]{:S(2)}) collective-permute-start(bf16[16,1,130]{2,0,1:T(8,128)(2,1)S(1)} %get-tuple-element.125), channel_id=1, source_target_pairs={{0,1},{1,2},{2,3},{4,5},{5,6},{6,7},{8,9},{9,10},{10,11},{12,13},{... | collective-permute-start | bytes 12488 | tf_op jit(solution)/shard_map/ppermute | solution.py:20
  358.9 7.7 %copy-start.2 = (bf16[16,1024,1]{2,0,1:T(8,128)(2,1)S(1)}, bf16[16,1024,1]{2,0,1:T(8,128)(2,1)}, u32[]{:S(2)}) copy-start(bf16[16,1024,1]{2,0,1:T(8,128)(2,1)} %copy.33) | copy-start | bytes 98308
  358.9 7.7 %collective-permute-start.5 = (bf16[16,1,130]{2,0,1:T(8,128)(2,1)S(1)}, bf16[16,1,130]{2,0,1:T(8,128)(2,1)S(1)}, u32[]{:S(2)}, u32[]{:S(2)}) collective-permute-start(bf16[16,1,130]{2,0,1:T(8,128)(2,1)S(1)} %get-tuple-element.126), channel_id=1, source_target_pairs={{1,0},{2,1},{3,2},{5,4},{6,5},{7,6},{9,8},{10,9},{11,10},{13,12},{... | collective-permute-start | bytes 12488 | tf_op jit(solution)/shard_map/ppermute | solution.py:22
  380.0 19.3 %copy-start.4 = (bf16[16,1025,130]{2,0,1:T(8,128)(2,1)}, bf16[16,1025,130]{2,0,1:T(8,128)(2,1)S(1)}, u32[]{:S(2)}) copy-start(bf16[16,1025,130]{2,0,1:T(8,128)(2,1)S(1)} %get-tuple-element.124) | copy-start | bytes 12792004
where the time goes:
time: 445 us; the launch traced here: 437 us
  matrix products  204 us (46%)
  waiting for transfers between devices  104 us (23%)
  local copies, waits for them, and re-layouts  50.9 us (11%)
  starting transfers between devices  41.2 us (9%)
  other arithmetic  35.7 us (8%)
    dot_general x27, matrix products, conv_taps(): jnp.einsum('oi,ihw->ohw', kernel, window, preferred_element_type=jnp.floa...  133 us
    all_to_all x1, waiting for transfers between devices, local(): lax.all_to_all(payload, ('cam', 'row'), split_axis=0, concat_axis=0, tile...  101 us
    dot_general x16, matrix products, shift_blocks(): jnp.einsum('eck,ekj->ecj', block_group, table, preferred_element_type=jnp...  58.6 us
    gather x1, local copies, waits for them, and re-layouts, local(): picked = jnp.take(blocks, send_block.reshape(entries), axis=0)  16.3 us
    concatenate x2, other arithmetic, with_halo(): jnp.concatenate([lax.ppermute(tail, axis, [(i, (i + 1) % count) for i in...  13.6 us
    ppermute x3, starting transfers between devices, with_halo(): lax.ppermute(tail, axis, [(i, (i + 1) % count) for i in range(ends)])  12.9 us
    dot_general x1, matrix products, local(): gathered = jnp.dot(onehot, incoming, preferred_element_type=jnp.float32)  11.3 us
    all_to_all x1, starting transfers between devices, local(): lax.all_to_all(payload, ('cam', 'row'), split_axis=0, concat_axis=0, tile...  11.1 us
  transfers between devices with their start and end apart: 8, of which 3 were waited for; matrix products, arithmetic and copies ran while one was open for 43% of the time, Pallas kernels for 0%

commit v1 on v0

v1 whole, which is shorter than its diff:
```python
import functools

import jax
import jax.numpy as jnp
from jax import lax
from jax.experimental import pallas as pl
from jax.experimental.pallas import tpu as pltpu
from jax.sharding import PartitionSpec as P

C = 16
W = 2048
TL = 128
CAP = 16
AR_DEV = 1024
PEERS = 128
ROWS = 32
F32 = jnp.float32
BF16 = jnp.bfloat16
MESH = pl.DeviceIdType.MESH
NT = (((1,), (1,)), ((), ()))


def iota(shape, dim):
    return lax.broadcasted_iota(jnp.int32, shape, dim)


def dot(a, b):
    return jnp.dot(a, b, preferred_element_type=F32)


def band(weight, m, k, out_of_m, in_of_k):
    pick = jnp.where(out_of_m(iota((m, C), 0))[0] == iota((m, C), 1), 1.0, 0.0).astype(BF16)
    rows = dot(pick, weight).astype(BF16)
    step = in_of_k(iota((m, k), 1))[1] - out_of_m(iota((m, k), 0))[1] + 1
    channel = in_of_k(iota((9 * C, k), 1))[0]
    source = iota((9 * C, k), 0)
    taps = []
    for b in range(3):
        total = jnp.zeros((m, k), F32)
        for a in range(3):
            spread = jnp.where(source == (3 * a + b) * C + channel, 1.0, 0.0).astype(BF16)
            total = total + jnp.where(step == a, dot(rows, spread), 0.0)
        taps.append(total.astype(BF16))
    return taps


def row_major(first):
    return lambda i: (i % C, i // C + first)


def channel_major(first):
    return lambda i: (i // 16, i % 16 + first)


def shift_add(left, mid, right):
    n = mid.shape[1]
    lane = iota(mid.shape, 1)
    a = jnp.where(lane == 0, 0.0, pltpu.roll(left, 1, 1))
    b = jnp.where(lane == n - 1, 0.0, pltpu.roll(right, n - 1, 1))
    return mid + a + b


def join_kernel(
    image, w1, w2, code, scale_rows, tiles,
    joined, above, below, side_cols, corners,
    band1, band1h, band2, part_a, part_b, part_g, hidden, feats,
    edge_out, edge_in, turned, outbox, inbox, scale_in, onehot, total, wsum, pick_cols, cols, side_in, col_in, row_in,
    edge_send, edge_recv, send_sem, recv_sem, ssend_sem, srecv_sem, hsend, hrecv,
):
    cam = lax.axis_index("cam")
    row = lax.axis_index("row")
    cams = lax.axis_size("cam")
    strips = lax.axis_size("row")
    me = cam * strips + row

    barrier = pltpu.get_barrier_semaphore()

    def greet(i, carry):
        p = lax.rem(me + i, PEERS)
        pl.semaphore_signal(barrier, inc=1, device_id=(p // strips, p % strips), device_id_type=MESH)
        return carry

    lax.fori_loop(1, PEERS, greet, 0)

    def edges(n, carry):
        at = pl.ds(pl.multiple_of(n * 256, 256), 256)
        for half in range(2):
            field = image[:, half * 16 : half * 16 + 16, at].reshape(256, 256)
            first = 14 if half == 1 else 0
            m, k = iota((32, 256), 0), iota((32, 256), 1)
            pick = jnp.where(k == (m % C) * 16 + first + m // C, 1.0, 0.0).astype(BF16)
            edge_out[half, :, at] = dot(pick, field).astype(BF16)
        return carry

    lax.fori_loop(0, W // 256, edges, 0)
    up = (cam, lax.rem(row + strips - 1, strips))
    down = (cam, lax.rem(row + 1, strips))
    pl.semaphore_wait(barrier, PEERS - 1)
    edge_copies = [
        pltpu.make_async_remote_copy(
            src_ref=edge_out.at[half], dst_ref=edge_in.at[half], send_sem=edge_send.at[half], recv_sem=edge_recv.at[half],
            device_id=where, device_id_type=MESH,
        )
        for half, where in ((0, up), (1, down))
    ]
    for copy in edge_copies:
        copy.start()

    for b, taps in enumerate(band(w1[...], 288, 256, row_major(-1), channel_major(0))):
        band1[b] = taps
    for b, taps in enumerate(band(w1[...], 32, 32, row_major(-1), row_major(-2))):
        band1h[0, b] = taps
    for b, taps in enumerate(band(w1[...], 32, 32, row_major(31), row_major(32))):
        band1h[1, b] = taps
    for b, taps in enumerate(band(w2[...], 224, 256, row_major(0), row_major(-1))):
        band2[b] = taps

    def first_main(n, carry):
        at = pl.ds(pl.multiple_of(n * 256, 256), 256)
        for half, part in ((0, part_a), (1, part_b)):
            field = image[:, half * 16 : half * 16 + 16, at].reshape(256, 256)
            for b in range(3):
                part[b, :, at] = dot(band1[b], field)
        return carry

    lax.fori_loop(0, W // 256, first_main, 0)

    def silu(v):
        return v / (1.0 + jnp.exp(-v))

    def hide(at, sources):
        taps = []
        for b in range(3):
            value = None
            for part, first in sources:
                term = part[b, pl.ds(first, 16), :]
                value = term if value is None else value + term
            taps.append(value)
        return silu(shift_add(*taps))

    def put(at, value):
        hidden[pl.ds(at, 16), :] = value.astype(BF16)

    def body_a(i, carry):
        at = pl.multiple_of(i * 16, 16)
        put(at, hide(i, [(part_a, at)]))
        return carry

    def body_b(i, carry):
        at = pl.multiple_of(i * 16, 16)
        put(at, hide(i, [(part_b, pl.multiple_of(at - 256, 16))]))
        return carry

    lax.fori_loop(2, 16, body_a, 0)
    for i in (16, 17):
        put(i * 16, hide(i, [(part_a, i * 16), (part_b, i * 16 - 256)]))
    lax.fori_loop(18, 32, body_b, 0)

    for copy in edge_copies:
        copy.wait()
    has_above = (row > 0).astype(F32)
    has_below = (row < strips - 1).astype(F32)
    above_bf = has_above.astype(BF16)
    below_bf = has_below.astype(BF16)

    def first_edge(n, carry):
        at = pl.ds(pl.multiple_of(n * 256, 256), 256)
        top = edge_in[1, :, at] * above_bf
        bottom = edge_in[0, :, at] * below_bf
        for b in range(3):
            part_g[b, 0:32, at] = dot(band1h[0, b], top)
            part_g[b, 32:64, at] = dot(band1h[1, b], bottom)
        return carry

    lax.fori_loop(0, W // 256, first_edge, 0)
    put(0, hide(0, [(part_a, 0), (part_g, 0)]) * has_above)
    put(16, hide(1, [(part_a, 16), (part_g, 16)]))
    put(512, hide(32, [(part_b, 256), (part_g, 32)]))
    put(528, hide(33, [(part_b, 272), (part_g, 48)]) * has_below)

    def second(n, carry):
        at = pl.ds(pl.multiple_of(n * 256, 256), 256)
        for b in range(3):
            part_a[b, 0:224, at] = dot(band2[b], hidden[0:256, at])
            part_b[b, 0:224, at] = dot(band2[b], hidden[224:480, at])
            part_g[b, :, at] = dot(band2[b, 0:64, 0:96], hidden[448:544, at])
        return carry

    lax.fori_loop(0, W // 256, second, 0)

    def feature_row(part, first):
        def body(i, carry):
            at = pl.ds(pl.multiple_of(i * 16, 16), 16)
            value = shift_add(part[0, at, :], part[1, at, :], part[2, at, :]).astype(BF16).astype(F32)
            for t in range(W // TL):
                feats[(first + i) * (W // TL) + t] = value[:, t * TL : (t + 1) * TL]
            return carry

        return body

    lax.fori_loop(0, 14, feature_row(part_a, 0), 0)
    lax.fori_loop(0, 14, feature_row(part_b, 14), 0)
    lax.fori_loop(0, 4, feature_row(part_g, 28), 0)

    zc = lax.rem(me, 8)
    unit = me // 8
    uy, ux = unit // 4, unit % 4

    def peer_of(step):
        d = lax.rem((step // 8) * 5, 16)
        k = step % 8
        u = lax.rem(uy + d // 4, 4) * 4 + lax.rem(ux + d % 4, 4)
        return u * 8 + lax.rem(zc // 4 + k // 4, 2) * 4 + lax.rem(zc % 4 + k % 4, 4)

    def make(p, slot, put_tile):
        for e in range(CAP):
            word = code[p * CAP + e]
            block = word & 511
            shift = (word >> 9) & 127
            scale = (word >> 16).astype(F32) * 0.0625
            turned[slot, e * C : (e + 1) * C, :] = pltpu.roll(feats[block], shift, 1) * scale
        for q in range(C):
            put_tile(q, turned[slot, pl.ds(q, CAP, stride=C), :].astype(BF16))

    def put_own(q, value):
        inbox[me, q] = value

    make(me, 0, put_own)
    scale_in[me] = scale_rows[me]

    def block_copy(p):
        return pltpu.make_async_remote_copy(
            src_ref=outbox.at[p], dst_ref=inbox.at[me], send_sem=send_sem, recv_sem=recv_sem.at[unit],
            device_id=(p // strips, p % strips), device_id_type=MESH,
        )

    def scale_copy(p):
        return pltpu.make_async_remote_copy(
            src_ref=scale_rows.at[p], dst_ref=scale_in.at[me], send_sem=ssend_sem, recv_sem=srecv_sem,
            device_id=(p // strips, p % strips), device_id_type=MESH,
        )

    def send_step(step, carry):
        p = peer_of(step)

        def put_tile(q, value):
            outbox[p, q] = value

        make(p, lax.rem(step, 2), put_tile)
        scale_copy(p).start()
        block_copy(p).start()
        return carry

    lax.fori_loop(1, PEERS, send_step, 0)

    def pick_body(q, carry):
        j, lane = iota((TL, 256), 0), iota((TL, 256), 1)
        hit = ((j == 0) & (lane == q)) | ((j == TL - 1) & (lane == q + TL))
        pick_cols[pl.ds(pl.multiple_of(q * TL, TL), TL), :] = jnp.where(hit, 1.0, 0.0).astype(BF16)
        return carry

    lax.fori_loop(0, C, pick_body, 0)

    def clear(i, carry):
        total[pl.ds(pl.multiple_of(i * 1024, 1024), 1024), :] = jnp.zeros((1024, TL), F32)
        return carry

    lax.fori_loop(0, C, clear, 0)
    wsum[...] = jnp.zeros_like(wsum)

    pltpu.make_async_remote_copy(
        src_ref=scale_rows.at[pl.ds(0, PEERS - 1)], dst_ref=scale_in.at[pl.ds(0, PEERS - 1)], send_sem=ssend_sem,
        recv_sem=srecv_sem, device_id=up, device_id_type=MESH,
    ).wait()

    def wait_unit(u, count):
        pltpu.make_async_remote_copy(
            src_ref=outbox.at[pl.ds(0, count)], dst_ref=inbox.at[pl.ds(0, count)], send_sem=send_sem,
            recv_sem=recv_sem.at[u], device_id=up, device_id_type=MESH,
        ).wait_recv()

    def source_unit(i):
        d = lax.rem(i * 5, 16)
        return lax.rem(uy + 4 - d // 4, 4) * 4 + lax.rem(ux + 4 - d % 4, 4)

    def add_pair(i):
        u, v = source_unit(2 * i), source_unit(2 * i + 1)
        ids = jnp.concatenate([tiles[pl.ds(u, 1), :], tiles[pl.ds(v, 1), :]], axis=1)
        weights = jnp.concatenate(
            [jnp.sum(scale_in[pl.ds(u * 8, 8)], axis=0), jnp.sum(scale_in[pl.ds(v * 8, 8)], axis=0)], axis=1
        )
        weights = jnp.broadcast_to(weights, (TL, 256)).astype(BF16)

        def mark(m, carry):
            at = pl.ds(pl.multiple_of(m * 256, 256), 256)
            hot = jnp.where(iota((256, 256), 0) + m * 256 == ids, 1.0, 0.0).astype(BF16)
            onehot[at, :] = hot
            wsum[at, :] += lax.dot_general(hot, weights, NT, preferred_element_type=F32)
            return carry

        lax.fori_loop(0, 4, mark, 0)

        def channels(t, carry):
            cols = []
            for q in (2 * t, 2 * t + 1):
                cols.append(
                    jnp.concatenate(
                        [inbox[pl.ds(u * 8, 8), q].reshape(TL, TL), inbox[pl.ds(v * 8, 8), q].reshape(TL, TL)], axis=0
                    )
                )
            block = jnp.concatenate(cols, axis=1)
            for m in range(4):
                got = dot(onehot[m * 256 : (m + 1) * 256, :], block)
                for h in range(2):
                    at = pl.ds(pl.multiple_of((2 * t + h) * AR_DEV + m * 256, 256), 256)
                    total[at, :] += got[:, h * TL : (h + 1) * TL]
            return carry

        lax.fori_loop(0, C // 2, channels, 0)

    wait_unit(source_unit(0), 7)
    wait_unit(source_unit(1), 8)
    add_pair(0)

    def receive(i, carry):
        wait_unit(source_unit(2 * i), 8)
        wait_unit(source_unit(2 * i + 1), 8)
        add_pair(i)
        return carry

    lax.fori_loop(1, 8, receive, 0)

    wsum[...] = 1.0 / jnp.maximum(wsum[...], 1.0)

    def ends(g, carry):
        for last in range(2):
            r = g * 16 + 15 * last
            value = (total[pl.ds(r, C, stride=AR_DEV), :] * wsum[pl.ds(r, 1), :]).astype(BF16)
            if last:
                above[g + 1] = value
            else:
                below[g] = value
        return carry

    lax.fori_loop(0, 64, ends, 0)

    def normal(rb, carry):
        at = pl.ds(pl.multiple_of(rb * TL, TL), TL)
        inverse = wsum[at, :]
        parts = []
        for q in range(C):
            value = (total[pl.ds(pl.multiple_of(q * AR_DEV + rb * TL, TL), TL), :] * inverse).astype(BF16)
            joined[q, at, :] = value
            parts.append(value)
        picked = dot(jnp.concatenate(parts, axis=1), pick_cols[...])
        left = pltpu.roll(picked[:, :TL], rb * C, 1)
        right = pltpu.roll(picked[:, TL:], rb * C, 1)
        return carry[0] + left, carry[1] + right

    zero = jnp.zeros((TL, TL), F32)
    left, right = lax.fori_loop(0, AR_DEV // TL, normal, (zero, zero))
    cols[0] = left.astype(BF16)
    cols[1] = right.astype(BF16)

    west, east = lax.rem(cam + cams - 1, cams), lax.rem(cam + 1, cams)
    north, south = lax.rem(row + strips - 1, strips), lax.rem(row + 1, strips)
    plan = [
        (cols.at[1], side_in.at[0], (east, row)),
        (cols.at[0], side_in.at[1], (west, row)),
        (above.at[64], row_in.at[0], (cam, south)),
        (below.at[0], row_in.at[1], (cam, north)),
        (cols.at[1, pl.ds(112, 16)], col_in.at[0], (east, south)),
        (cols.at[1, pl.ds(0, 16)], col_in.at[1], (east, north)),
        (cols.at[0, pl.ds(112, 16)], col_in.at[2], (west, south)),
        (cols.at[0, pl.ds(0, 16)], col_in.at[3], (west, north)),
    ]
    copies = [
        pltpu.make_async_remote_copy(
            src_ref=src, dst_ref=dst, send_sem=hsend.at[i], recv_sem=hrecv.at[i], device_id=where, device_id_type=MESH
        )
        for i, (src, dst, where) in enumerate(plan)
    ]
    for copy in copies:
        copy.start()
    pltpu.make_async_remote_copy(
        src_ref=outbox.at[pl.ds(0, PEERS - 1)], dst_ref=inbox.at[pl.ds(0, PEERS - 1)], send_sem=send_sem,
        recv_sem=recv_sem.at[0], device_id=up, device_id_type=MESH,
    ).wait_send()
    for copy in copies:
        copy.wait()
    has_west = (cam > 0).astype(F32)
    has_east = (cam < cams - 1).astype(F32)
    side_cols[0] = side_in[0] * has_west.astype(BF16)
    side_cols[1] = side_in[1] * has_east.astype(BF16)
    above[0] = row_in[0] * above_bf
    below[64] = row_in[1] * below_bf
    for i, factor in enumerate(
        (has_west * has_above, has_west * has_below, has_east * has_above, has_east * has_below)
    ):
        corners[i] = col_in[i] * factor.astype(BF16)


def uv_kernel(weight, joined, above, below, side_cols, corners, texture, bands, delta):
    rb = pl.program_id(0)

    @pl.when(rb == 0)
    def _():
        def out_of(i):
            return i // 16, i % 16

        def in_of(i):
            late = i - 256
            return (
                jnp.where(i < 256, i // 16, late % C),
                jnp.where(i < 256, i % 16, jnp.where(late < C, -1, 16)),
            )

        for b, taps in enumerate(band(weight[...], 256, 288, out_of, in_of)):
            bands[b * 256 : (b + 1) * 256, :] = taps

        lane = iota((TL, TL), 1)
        sub = iota((TL, TL), 0)
        pick = jnp.where(iota((TL, C), 0) % C == iota((TL, C), 1), 1.0, 0.0).astype(BF16)
        rows = dot(pick, weight[...]).astype(BF16)
        for side in range(2):
            own = side_cols[side].astype(F32)
            top = corners[2 * side].astype(F32)[15:16, :]
            bottom = corners[2 * side + 1].astype(F32)[0:1, :]
            before = jnp.where(lane[0:1] >= TL - C, top, own[TL - 1 : TL, :])
            before = pltpu.roll(jnp.broadcast_to(before, (TL, TL)), C, 1)
            after = jnp.where(lane[0:1] < C, bottom, own[0:1, :])
            after = pltpu.roll(jnp.broadcast_to(after, (TL, TL)), TL - C, 1)
            shifted = (
                jnp.where(sub == 0, before, pltpu.roll(own, 1, 0)),
                own,
                jnp.where(sub == TL - 1, after, pltpu.roll(own, TL - 1, 0)),
            )
            result = jnp.zeros((TL, TL), F32)
            for a in range(3):
                source = iota((9 * C, TL), 0)
                spread = jnp.where(source == (3 * a + 2 * side) * C + iota((9 * C, TL), 1) % C, 1.0, 0.0).astype(BF16)
                matrix = jnp.where(sub // C == lane // C, dot(rows, spread), 0.0).astype(BF16)
                result = result + lax.dot_general(shifted[a].astype(BF16), matrix, NT, preferred_element_type=F32)
            delta[side] = result

    turn = lax.rem(TL - rb * C, TL)
    left = pltpu.roll(delta[0], turn, 1)
    right = pltpu.roll(delta[1], turn, 1)
    lane = iota((16, TL), 1)
    for pair in range(4):
        fields = []
        for h in range(2):
            g = pair * 2 + h
            at = rb * 8 + g
            fields.append(
                jnp.concatenate(
                    [joined[:, g * 16 : (g + 1) * 16, :].reshape(256, TL), above[at], below[at + 1]], axis=0
                )
            )
        taps = dot(bands[...], jnp.concatenate(fields, axis=1))
        for h in range(2):
            g = pair * 2 + h
            cut = slice(h * TL, (h + 1) * TL)
            a = pltpu.roll(taps[0:256, cut], 1, 1)
            m = taps[256:512, cut]
            b = pltpu.roll(taps[512:768, cut], TL - 1, 1)
            for o in range(C):
                rows = slice(o * 16, (o + 1) * 16)
                here = slice(g * 16, (g + 1) * 16)
                low = jnp.where(lane == 0, left[here, o : o + 1], a[rows])
                high = jnp.where(lane == TL - 1, right[here, o : o + 1], b[rows])
                value = joined[o, here, :].astype(F32) + m[rows] + low + high
                texture[o, here, :] = value.astype(BF16)


def local(image, conv_first, conv_second, conv_uv, send_block, send_shift, send_weight, send_count, recv_tile):
    me = lax.axis_index("cam") * lax.axis_size("row") + lax.axis_index("row")
    block = send_block.reshape(PEERS, CAP)
    shift = send_shift.reshape(PEERS, CAP)
    valid = lax.broadcasted_iota(jnp.int32, (PEERS, CAP), 1) < send_count.reshape(PEERS, 1)
    weight = jnp.where(valid, send_weight.reshape(PEERS, CAP), 0)
    code = (block + shift * 512 + weight * 65536).reshape(PEERS * CAP)
    scale = weight.astype(F32) * 0.0625
    lane = lax.broadcasted_iota(jnp.int32, (PEERS, TL), 1)
    scale_rows = jnp.where(lane // CAP == me % 8, jnp.tile(scale, (1, 8)), 0.0).reshape(PEERS, 1, TL)
    tiles = recv_tile.reshape(16, TL)

    vmem = pl.BlockSpec(memory_space=pltpu.VMEM)
    smem = pl.BlockSpec(memory_space=pltpu.SMEM)
    dma = pltpu.SemaphoreType.DMA
    joined, above, below, side_cols, corners = pl.pallas_call(
        join_kernel,
        out_shape=[
            jax.ShapeDtypeStruct((C, AR_DEV, TL), BF16),
            jax.ShapeDtypeStruct((65, C, TL), BF16),
            jax.ShapeDtypeStruct((65, C, TL), BF16),
            jax.ShapeDtypeStruct((2, TL, TL), BF16),
            jax.ShapeDtypeStruct((4, 16, TL), BF16),
        ],
        in_specs=[vmem, vmem, vmem, smem, vmem, vmem],
        out_specs=[vmem] * 5,
        scratch_shapes=[
            pltpu.VMEM((3, 288, 256), BF16),
            pltpu.VMEM((2, 3, 32, 32), BF16),
            pltpu.VMEM((3, 224, 256), BF16),
            pltpu.VMEM((3, 288, W), F32),
            pltpu.VMEM((3, 288, W), F32),
            pltpu.VMEM((3, 64, W), F32),
            pltpu.VMEM((544, W), BF16),
            pltpu.VMEM((512, C, TL), F32),
            pltpu.VMEM((2, 32, W), BF16),
            pltpu.VMEM((2, 32, W), BF16),
            pltpu.VMEM((2, CAP * C, TL), F32),
            pltpu.VMEM((PEERS, C, CAP, TL), BF16),
            pltpu.VMEM((PEERS, C, CAP, TL), BF16),
            pltpu.VMEM((PEERS, 1, TL), F32),
            pltpu.VMEM((AR_DEV, 256), BF16),
            pltpu.VMEM((C * AR_DEV, TL), F32),
            pltpu.VMEM((AR_DEV, TL), F32),
            pltpu.VMEM((C * TL, 256), BF16),
            pltpu.VMEM((2, TL, TL), BF16),
            pltpu.VMEM((2, TL, TL), BF16),
            pltpu.VMEM((4, 16, TL), BF16),
            pltpu.VMEM((2, C, TL), BF16),
            dma((2,)), dma((2,)), dma, dma((16,)), dma, dma, dma((8,)), dma((8,)),
        ],
        compiler_params=pltpu.CompilerParams(
            collective_id=0, has_side_effects=True, vmem_limit_bytes=62 * 1024 * 1024
        ),
        cost_estimate=pl.CostEstimate(flops=2 * 10**10, bytes_accessed=3 * 10**7, transcendentals=10**6),
    )(image.reshape(C, ROWS, W), conv_first, conv_second, code, scale_rows, tiles)

    full = lambda shape: pl.BlockSpec(shape, lambda i: (0,) * len(shape))
    return pl.pallas_call(
        uv_kernel,
        out_shape=jax.ShapeDtypeStruct((C, AR_DEV, TL), BF16),
        grid=(AR_DEV // TL,),
        in_specs=[
            full((C, 9 * C)),
            pl.BlockSpec((C, TL, TL), lambda i: (0, i, 0)),
            full((65, C, TL)),
            full((65, C, TL)),
            full((2, TL, TL)),
            full((4, 16, TL)),
        ],
        out_specs=pl.BlockSpec((C, TL, TL), lambda i: (0, i, 0)),
        scratch_shapes=[pltpu.VMEM((768, 288), BF16), pltpu.VMEM((2, TL, TL), F32)],
        compiler_params=pltpu.CompilerParams(vmem_limit_bytes=32 * 1024 * 1024),
        cost_estimate=pl.CostEstimate(flops=10**10, bytes_accessed=10**7, transcendentals=0),
    )(conv_uv, joined, above, below, side_cols, corners)


def solution(mesh):
    return jax.shard_map(
        local,
        mesh=mesh,
        in_specs=(
            P("cam", None, "row", None),
            P(),
            P(),
            P(),
            P("cam", "row", None, None),
            P("cam", "row", None, None),
            P("cam", "row", None, None),
            P("cam", "row", None),
            P("row", "cam", None, None),
        ),
        out_specs=P(None, "row", "cam"),
        check_vma=False,
    )
```

time: 445 us -> 243 us (0.55)
  the two profiles are of different devices: /device:TPU:47 before, /device:TPU:1 now
where the time goes in v1:
time: 243 us; the launch traced here: 241 us
  Pallas kernels  229 us (94%)
  local copies, waits for them, and re-layouts  8.49 us (3%)
  other arithmetic  3.41 us (1%)
    pallas_call x1, Pallas kernels, local(): pl.pallas_call(join_kernel, out_shape=[jax.ShapeDtypeStruct((C, AR_DEV, T...  214 us
    pallas_call x1, Pallas kernels, local(): pl.pallas_call(uv_kernel, out_shape=jax.ShapeDtypeStruct((C, AR_DEV, TL),...  15.1 us
    unnamed x14, local copies, waits for them, and re-layouts  7.24 us

profile of v1, /device:TPU:1, one launch (start us, length us, event | category | flops | bytes accessed | tf_op | source)
XLA Modules:
  0.0 240.9 jit_solution(16214370904319564790)
XLA Ops:
  0.0 0.7 iota_compare_fusion
  0.7 0.7 multiply_add_fusion.1
  1.4 0.7 fusion.1
  2.1 0.1 copy.13
  2.2 0.1 lt.27
  2.3 0.1 copy.15
  2.4 0.7 compare_select_fusion.scale_rows
  3.1 0.1 copy.12
  3.2 0.1 add.21
  3.3 0.8 copy.16
  4.1 0.7 reshape.126.tiles
  4.8 0.8 copy.14
  5.6 0.1 reshape.124
  5.7 0.6 multiply_add_fusion.code
  6.3 0.0 copy-start
  6.3 213.8 %shard_map.91 = (bf16[16,1024,128]{2,1,0:T(8,128)(2,1)}, bf16[65,16,128]{2,1,0:T(8,128)(2,1)}, bf16[65,16,128]{2,1,0:T(8,128)(2,1)}, bf16[2,128,128]{2,1,0:T(8,128)(2,1)}, bf16[4,16,128]{2,1,0:T(8,128)(2,1)}) custom-call(bf16[16,32,2048]{2,1,0:T(8,128)(2,1)} %bitcast.18, bf16[16,144]{1,0:T(8,128)(2,1)} %w1.1, bf16[16,144]{1,0:T(8,128)(2,1)} %w2.1, ...), custom_call_target="tpu_custom_call" | custom-call | flops 20000000000 | bytes 30000000 | tf_op jit(solution)/shard_map/pallas_call | solution.py:491
  220.1 0.0 copy-done
  220.1 0.0 copy-start.1
  220.2 2.2 copy-done.1
  222.3 0.0 copy-start.2
  222.3 0.9 copy-done.2
  223.3 0.0 copy-start.3
  223.3 0.9 copy-done.3
  224.2 0.0 copy-start.4
  224.2 0.8 copy-done.4
  225.1 0.0 copy-start.5
  225.1 0.7 copy-done.5
  225.8 15.1 %shard_map.92 = bf16[16,1024,128]{2,1,0:T(8,128)(2,1)} custom-call(bf16[16,144]{1,0:T(8,128)(2,1)S(1)} %copy-done, bf16[16,1024,128]{2,1,0:T(8,128)(2,1)S(1)} %copy-done.1, bf16[65,16,128]{2,1,0:T(8,128)(2,1)S(1)} %copy-done.2, bf16[65,16,128]{2,1,0:T(8,128)(2,1)S(1)} %copy-done.3, bf16[2,128,128]{2,1,0:T(8,128)(2,1)S(1)} %copy-done.4, ...), custom_call_target="tpu_custom_call" | custom-call | flops 10000000000 | bytes 10000000 | tf_op jit(solution)/shard_map/pallas_call | solution.py:534
  (3 shorter events, 0.0 us)
Async XLA Ops:
  6.3 213.9 %copy-start = (bf16[16,144]{1,0:T(8,128)(2,1)S(1)}, bf16[16,144]{1,0:T(8,128)(2,1)}, u32[]{:S(2)}) copy-start(bf16[16,144]{1,0:T(8,128)(2,1)} %weight.1) | copy-start | bytes 13828
  220.1 2.2 copy-start.1
  222.3 1.0 copy-start.2
  223.3 1.0 copy-start.3
  224.2 0.8 copy-start.4
  225.1 0.7 copy-start.5

commit v2 on v1

--- a/solution.py
+++ b/solution.py
@@ -13,6 +13,7 @@
 CAP = 16
 AR_DEV = 1024
 PEERS = 128
+GROUP = 16
 ROWS = 32
 F32 = jnp.float32
 BF16 = jnp.bfloat16
@@ -95,6 +96,24 @@
     lax.fori_loop(0, W // 256, edges, 0)
     up = (cam, lax.rem(row + strips - 1, strips))
     down = (cam, lax.rem(row + 1, strips))
+    for b, taps in enumerate(band(w1[...], 288, 256, row_major(-1), channel_major(0))):
+        band1[b] = taps
+    for b, taps in enumerate(band(w1[...], 32, 32, row_major(-1), row_major(-2))):
+        band1h[0, b] = taps
+    for b, taps in enumerate(band(w1[...], 32, 32, row_major(31), row_major(32))):
+        band1h[1, b] = taps
+    for b, taps in enumerate(band(w2[...], 224, 256, row_major(0), row_major(-1))):
+        band2[b] = taps
+
+    def first_main(n, carry):
+        at = pl.ds(pl.multiple_of(n * 256, 256), 256)
+        for half, part in ((0, part_a), (1, part_b)):
+            field = image[:, half * 16 : half * 16 + 16, at].reshape(256, 256)
+            for b in range(3):
+                part[b, :, at] = dot(band1[b], field)
+        return carry
+
+    lax.fori_loop(0, W // 256, first_main, 0)
     pl.semaphore_wait(barrier, PEERS - 1)
     edge_copies = [
         pltpu.make_async_remote_copy(
@@ -106,24 +125,6 @@
     for copy in edge_copies:
         copy.start()
 
-    for b, taps in enumerate(band(w1[...], 288, 256, row_major(-1), channel_major(0))):
-        band1[b] = taps
-    for b, taps in enumerate(band(w1[...], 32, 32, row_major(-1), row_major(-2))):
-        band1h[0, b] = taps
-    for b, taps in enumerate(band(w1[...], 32, 32, row_major(31), row_major(32))):
-        band1h[1, b] = taps
-    for b, taps in enumerate(band(w2[...], 224, 256, row_major(0), row_major(-1))):
-        band2[b] = taps
-
-    def first_main(n, carry):
-        at = pl.ds(pl.multiple_of(n * 256, 256), 256)
-        for half, part in ((0, part_a), (1, part_b)):
-            field = image[:, half * 16 : half * 16 + 16, at].reshape(256, 256)
-            for b in range(3):
-                part[b, :, at] = dot(band1[b], field)
-        return carry
-
-    lax.fori_loop(0, W // 256, first_main, 0)
 
     def silu(v):
         return v / (1.0 + jnp.exp(-v))
@@ -202,15 +203,28 @@
     lax.fori_loop(0, 14, feature_row(part_b, 14), 0)
     lax.fori_loop(0, 4, feature_row(part_g, 28), 0)
 
-    zc = lax.rem(me, 8)
-    unit = me // 8
-    uy, ux = unit // 4, unit % 4
-
-    def peer_of(step):
-        d = lax.rem((step // 8) * 5, 16)
-        k = step % 8
-        u = lax.rem(uy + d // 4, 4) * 4 + lax.rem(ux + d % 4, 4)
-        return u * 8 + lax.rem(zc // 4 + k // 4, 2) * 4 + lax.rem(zc % 4 + k % 4, 4)
+    my, mx, mc = cam // 8, lax.rem(cam // 2, 4), lax.rem(cam, 2)
+
+    def offset(t):
+        i, c, b = t % 4, (t // 8) % 4, t // 32
+
+        def order(v):
+            w = lax.rem(v, 4)
+            return lax.rem(2 * w, 3) + 3 * (w // 3)
+
+        return order(i + b), order(i), (t // 4) % 2, order(i + c)
+
+    def moved(core, sign, t):
+        dy, dx, _, dz = offset(t)
+        place = (lax.rem(my + 4 + sign * dy, 4) * 4 + lax.rem(mx + 4 + sign * dx, 4)) * 2 + core
+        return place * 4 + lax.rem(row + 4 + sign * dz, 4)
+
+    def peer_of(t):
+        return moved(lax.rem(mc + offset(t)[2], 2), 1 - 2 * mc, t)
+
+    def source_of(t):
+        core = lax.rem(mc + offset(t)[2], 2)
+        return moved(core, 2 * core - 1, t)
 
     def make(p, slot, put_tile):
         for e in range(CAP):
@@ -223,32 +237,33 @@
             put_tile(q, turned[slot, pl.ds(q, CAP, stride=C), :].astype(BF16))
 
     def put_own(q, value):
-        inbox[me, q] = value
+        inbox[0, q] = value
 
     make(me, 0, put_own)
-    scale_in[me] = scale_rows[me]
-
-    def block_copy(p):
+    scale_in[0] = scale_rows[me]
+
+    def block_copy(t, p):
         return pltpu.make_async_remote_copy(
-            src_ref=outbox.at[p], dst_ref=inbox.at[me], send_sem=send_sem, recv_sem=recv_sem.at[unit],
+            src_ref=outbox.at[t], dst_ref=inbox.at[t], send_sem=send_sem,
+            recv_sem=recv_sem.at[t // GROUP], device_id=(p // strips, p % strips), device_id_type=MESH,
+        )
+
+    def scale_copy(t, p):
+        return pltpu.make_async_remote_copy(
+            src_ref=scale_rows.at[p], dst_ref=scale_in.at[t], send_sem=ssend_sem, recv_sem=srecv_sem,
             device_id=(p // strips, p % strips), device_id_type=MESH,
         )
 
-    def scale_copy(p):
-        return pltpu.make_async_remote_copy(
-            src_ref=scale_rows.at[p], dst_ref=scale_in.at[me], send_sem=ssend_sem, recv_sem=srecv_sem,
-            device_id=(p // strips, p % strips), device_id_type=MESH,
-        )
-
-    def send_step(step, carry):
-        p = peer_of(step)
+    def send_step(t, carry):
+        p = peer_of(t)
 
         def put_tile(q, value):
-            outbox[p, q] = value
-
-        make(p, lax.rem(step, 2), put_tile)
-        scale_copy(p).start()
-        block_copy(p).start()
+            outbox[t, q] = value
+
+        make(p, lax.rem(t, 2), put_tile)
+
+        scale_copy(t, p).start()
+        block_copy(t, p).start()
         return carry
 
     lax.fori_loop(1, PEERS, send_step, 0)
@@ -268,74 +283,88 @@
     lax.fori_loop(0, C, clear, 0)
     wsum[...] = jnp.zeros_like(wsum)
 
+    def wait_group(g, count):
+        pltpu.make_async_remote_copy(
+            src_ref=outbox.at[pl.ds(0, count)], dst_ref=inbox.at[pl.ds(0, count)], send_sem=send_sem,
+            recv_sem=recv_sem.at[g], device_id=up, device_id_type=MESH,
+        ).wait_recv()
+
+    def lanes_of(ref, g, half):
+        first = g * GROUP + half * 8
+        lane = iota((1, TL), 1) // CAP
+        value = jnp.zeros((1, TL), ref.dtype)
+        for i in range(8):
+            index = first + i if ref is scale_in else source_of(first + i)
+            value = jnp.where(lane == i, ref[index], value)
+        return value
+
+    def mark_group(g, carry):
+        ids = jnp.concatenate([lanes_of(tiles, g, 0), lanes_of(tiles, g, 1)], axis=1)
+        for m in range(4):
+            hot = jnp.where(iota((256, 256), 0) + m * 256 == ids, 1.0, 0.0).astype(BF16)
+            onehot[g, m * 256 : (m + 1) * 256, :] = hot
+        return carry
+
+    def weigh_group(g, carry):
+        weights = jnp.concatenate([lanes_of(scale_in, g, 0), lanes_of(scale_in, g, 1)], axis=1)
+        weights = jnp.broadcast_to(weights, (TL, 256)).astype(BF16)
+        for m in range(4):
+            at = slice(m * 256, (m + 1) * 256)
+            wsum[at, :] += lax.dot_general(onehot[g, at, :], weights, NT, preferred_element_type=F32)
+        return carry
+
+    def group_sum(g, t, m):
+        block = jnp.concatenate(
+            [inbox[pl.ds(g * GROUP, GROUP), 2 * t + h].reshape(256, TL) for h in range(2)], axis=1
+        )
+        return dot(onehot[g, m * 256 : (m + 1) * 256, :], block)
+
+    def add_group(g):
+        def channels(t, carry):
+            for m in range(4):
+                got = group_sum(g, t, m)
+                for h in range(2):
+                    at = pl.ds(pl.multiple_of((2 * t + h) * AR_DEV + m * 256, 256), 256)
+                    total[at, :] += got[:, h * TL : (h + 1) * TL]
+            return carry
+
+        lax.fori_loop(0, C // 2, channels, 0)
+
+    lax.fori_loop(0, PEERS // GROUP, mark_group, 0)
+    wait_group(0, GROUP - 1)
+    add_group(0)
+
+    def receive(g, carry):
+        wait_group(g, GROUP)
+        add_group(g)
+        return carry
+
+    last = PEERS // GROUP - 1
+    lax.fori_loop(1, last, receive, 0)
     pltpu.make_async_remote_copy(
         src_ref=scale_rows.at[pl.ds(0, PEERS - 1)], dst_ref=scale_in.at[pl.ds(0, PEERS - 1)], send_sem=ssend_sem,
         recv_sem=srecv_sem, device_id=up, device_id_type=MESH,
     ).wait()
-
-    def wait_unit(u, count):
-        pltpu.make_async_remote_copy(
-            src_ref=outbox.at[pl.ds(0, count)], dst_ref=inbox.at[pl.ds(0, count)], send_sem=send_sem,
-            recv_sem=recv_sem.at[u], device_id=up, device_id_type=MESH,
-        ).wait_recv()
-
-    def source_unit(i):
-        d = lax.rem(i * 5, 16)
-        return lax.rem(uy + 4 - d // 4, 4) * 4 + lax.rem(ux + 4 - d % 4, 4)
-
-    def add_pair(i):
-        u, v = source_unit(2 * i), source_unit(2 * i + 1)
-        ids = jnp.concatenate([tiles[pl.ds(u, 1), :], tiles[pl.ds(v, 1), :]], axis=1)
-        weights = jnp.concatenate(
-            [jnp.sum(scale_in[pl.ds(u * 8, 8)], axis=0), jnp.sum(scale_in[pl.ds(v * 8, 8)], axis=0)], axis=1
-        )
-        weights = jnp.broadcast_to(weights, (TL, 256)).astype(BF16)
-
-        def mark(m, carry):
-            at = pl.ds(pl.multiple_of(m * 256, 256), 256)
-            hot = jnp.where(iota((256, 256), 0) + m * 256 == ids, 1.0, 0.0).astype(BF16)
-            onehot[at, :] = hot
-            wsum[at, :] += lax.dot_general(hot, weights, NT, preferred_element_type=F32)
-            return carry
-
-        lax.fori_loop(0, 4, mark, 0)
-
-        def channels(t, carry):
-            cols = []
-            for q in (2 * t, 2 * t + 1):
-                cols.append(
-                    jnp.concatenate(
-                        [inbox[pl.ds(u * 8, 8), q].reshape(TL, TL), inbox[pl.ds(v * 8, 8), q].reshape(TL, TL)], axis=0
-                    )
-                )
-            block = jnp.concatenate(cols, axis=1)
-            for m in range(4):
-                got = dot(onehot[m * 256 : (m + 1) * 256, :], block)
-                for h in range(2):
-                    at = pl.ds(pl.multiple_of((2 * t + h) * AR_DEV + m * 256, 256), 256)
-                    total[at, :] += got[:, h * TL : (h + 1) * TL]
-            return carry
-
-        lax.fori_loop(0, C // 2, channels, 0)
-
-    wait_unit(source_unit(0), 7)
-    wait_unit(source_unit(1), 8)
-    add_pair(0)
-
-    def receive(i, carry):
-        wait_unit(source_unit(2 * i), 8)
-        wait_unit(source_unit(2 * i + 1), 8)
-        add_pair(i)
-        return carry
-
-    lax.fori_loop(1, 8, receive, 0)
-
+    lax.fori_loop(0, PEERS // GROUP, weigh_group, 0)
     wsum[...] = 1.0 / jnp.maximum(wsum[...], 1.0)
+    wait_group(last, GROUP)
+
+    def finish(t, carry):
+        for m in range(4):
+            got = group_sum(last, t, m)
+            for h in range(2):
+                at = pl.ds(pl.multiple_of((2 * t + h) * AR_DEV + m * 256, 256), 256)
+                value = (total[at, :] + got[:, h * TL : (h + 1) * TL]) * wsum[m * 256 : (m + 1) * 256, :]
+                total[at, :] = value
+                joined[2 * t + h, m * 256 : (m + 1) * 256, :] = value.astype(BF16)
+        return carry
+
+    lax.fori_loop(0, C // 2, finish, 0)
 
     def ends(g, carry):
         for last in range(2):
             r = g * 16 + 15 * last
-            value = (total[pl.ds(r, C, stride=AR_DEV), :] * wsum[pl.ds(r, 1), :]).astype(BF16)
+            value = total[pl.ds(r, C, stride=AR_DEV), :].astype(BF16)
             if last:
                 above[g + 1] = value
             else:
@@ -346,12 +375,7 @@
 
     def normal(rb, carry):
         at = pl.ds(pl.multiple_of(rb * TL, TL), TL)
-        inverse = wsum[at, :]
-        parts = []
-        for q in range(C):
-            value = (total[pl.ds(pl.multiple_of(q * AR_DEV + rb * TL, TL), TL), :] * inverse).astype(BF16)
-            joined[q, at, :] = value
-            parts.append(value)
+        parts = [joined[q, at, :] for q in range(C)]
         picked = dot(jnp.concatenate(parts, axis=1), pick_cols[...])
         left = pltpu.roll(picked[:, :TL], rb * C, 1)
         right = pltpu.roll(picked[:, TL:], rb * C, 1)
@@ -474,16 +498,14 @@
 
 
 def local(image, conv_first, conv_second, conv_uv, send_block, send_shift, send_weight, send_count, recv_tile):
-    me = lax.axis_index("cam") * lax.axis_size("row") + lax.axis_index("row")
     block = send_block.reshape(PEERS, CAP)
     shift = send_shift.reshape(PEERS, CAP)
     valid = lax.broadcasted_iota(jnp.int32, (PEERS, CAP), 1) < send_count.reshape(PEERS, 1)
     weight = jnp.where(valid, send_weight.reshape(PEERS, CAP), 0)
     code = (block + shift * 512 + weight * 65536).reshape(PEERS * CAP)
     scale = weight.astype(F32) * 0.0625
-    lane = lax.broadcasted_iota(jnp.int32, (PEERS, TL), 1)
-    scale_rows = jnp.where(lane // CAP == me % 8, jnp.tile(scale, (1, 8)), 0.0).reshape(PEERS, 1, TL)
-    tiles = recv_tile.reshape(16, TL)
+    scale_rows = jnp.tile(scale, (1, 8)).reshape(PEERS, 1, TL)
+    tiles = jnp.tile(recv_tile.reshape(PEERS, CAP), (1, 8)).reshape(PEERS, 1, TL)
 
     vmem = pl.BlockSpec(memory_space=pltpu.VMEM)
     smem = pl.BlockSpec(memory_space=pltpu.SMEM)
@@ -514,7 +536,7 @@
             pltpu.VMEM((PEERS, C, CAP, TL), BF16),
             pltpu.VMEM((PEERS, C, CAP, TL), BF16),
             pltpu.VMEM((PEERS, 1, TL), F32),
-            pltpu.VMEM((AR_DEV, 256), BF16),
+            pltpu.VMEM((PEERS // GROUP, AR_DEV, 256), BF16),
             pltpu.VMEM((C * AR_DEV, TL), F32),
             pltpu.VMEM((AR_DEV, TL), F32),
             pltpu.VMEM((C * TL, 256), BF16),
@@ -522,7 +544,7 @@
             pltpu.VMEM((2, TL, TL), BF16),
             pltpu.VMEM((4, 16, TL), BF16),
             pltpu.VMEM((2, C, TL), BF16),
-            dma((2,)), dma((2,)), dma, dma((16,)), dma, dma, dma((8,)), dma((8,)),
+            dma((2,)), dma((2,)), dma, dma((PEERS // GROUP,)), dma, dma, dma((8,)), dma((8,)),
         ],
         compiler_params=pltpu.CompilerParams(
             collective_id=0, has_side_effects=True, vmem_limit_bytes=62 * 1024 * 1024
@@ -545,7 +567,7 @@
         ],
         out_specs=pl.BlockSpec((C, TL, TL), lambda i: (0, i, 0)),
         scratch_shapes=[pltpu.VMEM((768, 288), BF16), pltpu.VMEM((2, TL, TL), F32)],
-        compiler_params=pltpu.CompilerParams(vmem_limit_bytes=32 * 1024 * 1024),
+        compiler_params=pltpu.CompilerParams(vmem_limit_bytes=62 * 1024 * 1024),
         cost_estimate=pl.CostEstimate(flops=10**10, bytes_accessed=10**7, transcendentals=0),
     )(conv_uv, joined, above, below, side_cols, corners)
 

time: 243 us -> 174 us (0.72)
  Pallas kernels: 229 us -> 165 us
  local copies, waits for them, and re-layouts: 8.49 us -> 3.44 us
    pallas_call x1, Pallas kernels: 214 us -> 149 us  [local(): pl.pallas_call(join_kernel, out_shape=[jax.ShapeDtypeStruct((C, AR_DEV, T...]
    unnamed x14 -> x1, local copies, waits for them, and re-layouts: 7.24 us -> 0.79 us
where the time goes in v2:
time: 174 us; the launch traced here: 171 us
  Pallas kernels  165 us (95%)
  local copies, waits for them, and re-layouts  3.44 us (2%)
  other arithmetic  2.69 us (2%)
    pallas_call x1, Pallas kernels, local(): pl.pallas_call(join_kernel, out_shape=[jax.ShapeDtypeStruct((C, AR_DEV, T...  149 us
    pallas_call x1, Pallas kernels, local(): pl.pallas_call(uv_kernel, out_shape=jax.ShapeDtypeStruct((C, AR_DEV, TL),...  16.3 us

profile of v2, /device:TPU:1, one launch (start us, length us, event | category | flops | bytes accessed | tf_op | source)
XLA Modules:
  0.0 171.2 jit_solution(3663737089300713498)
XLA Ops:
  0.0 0.7 iota_compare_fusion
  0.7 0.7 multiply_add_fusion.1
  1.4 0.7 fusion.1
  2.1 0.1 copy.13
  2.2 0.1 lt.21
  2.3 0.7 copy.15.scale_rows
  3.1 0.1 copy.12
  3.2 0.1 add.12
  3.2 0.7 tile.20
  3.9 0.7 copy.16.tiles
  4.7 0.8 copy.14
  5.5 0.1 reshape.58
  5.5 0.6 multiply_add_fusion.code
  6.1 148.7 %shard_map.91 = (bf16[16,1024,128]{2,1,0:T(8,128)(2,1)}, bf16[65,16,128]{2,1,0:T(8,128)(2,1)}, bf16[65,16,128]{2,1,0:T(8,128)(2,1)}, bf16[2,128,128]{2,1,0:T(8,128)(2,1)}, bf16[4,16,128]{2,1,0:T(8,128)(2,1)}) custom-call(bf16[16,32,2048]{2,1,0:T(8,128)(2,1)} %bitcast.20, bf16[16,144]{1,0:T(8,128)(2,1)} %w1.1, bf16[16,144]{1,0:T(8,128)(2,1)} %w2.1, ...), custom_call_target="tpu_custom_call" | custom-call | flops 20000000000 | bytes 30000000 | tf_op jit(solution)/shard_map/pallas_call | solution.py:513
  154.9 16.3 %shard_map.92 = bf16[16,1024,128]{2,1,0:T(8,128)(2,1)} custom-call(bf16[16,144]{1,0:T(8,128)(2,1)} %weight.1, bf16[16,1024,128]{2,1,0:T(8,128)(2,1)} %get-tuple-element.10.joined, bf16[65,16,128]{2,1,0:T(8,128)(2,1)} %get-tuple-element.11.above, bf16[65,16,128]{2,1,0:T(8,128)(2,1)} %get-tuple-element.12.below, ...), custom_call_target="tpu_custom_call" | custom-call | flops 10000000000 | bytes 10000000 | tf_op jit(solution)/shard_map/pallas_call | solution.py:556
  (1 shorter events, 0.0 us)

commit v3 on v2

--- a/solution.py
+++ b/solution.py
@@ -62,11 +62,12 @@
 
 
 def join_kernel(
-    image, w1, w2, code, scale_rows, tiles,
-    joined, above, below, side_cols, corners,
+    image, w1, w2, wuv, code, scale_rows, tiles,
+    texture,
+    joined, above, below, band_uv, side_mats, spread_mat, side_parts, col_sum,
     band1, band1h, band2, part_a, part_b, part_g, hidden, feats,
     edge_out, edge_in, turned, outbox, inbox, scale_in, onehot, total, wsum, pick_cols, cols, side_in, col_in, row_in,
-    edge_send, edge_recv, send_sem, recv_sem, ssend_sem, srecv_sem, hsend, hrecv,
+    edge_send, edge_recv, send_sem, recv_sem, ssend_sem, srecv_sem, hsend, hrecv, out_sem,
 ):
     cam = lax.axis_index("cam")
     row = lax.axis_index("row")
@@ -282,6 +283,34 @@
 
     lax.fori_loop(0, C, clear, 0)
     wsum[...] = jnp.zeros_like(wsum)
+    col_sum[...] = jnp.zeros_like(col_sum)
+
+    def uv_in(i):
+        late = i - 256
+        return (
+            jnp.where(i < 256, i // 16, late % C),
+            jnp.where(i < 256, i % 16, jnp.where(late < C, -1, 16)),
+        )
+
+    for b, taps in enumerate(band(wuv[...], 256, 288, channel_major(0), uv_in)):
+        band_uv[b * 256 : (b + 1) * 256, :] = taps
+
+    lane = iota((TL, TL), 1)
+    sub = iota((TL, TL), 0)
+    pick = jnp.where(iota((TL, C), 0) % C == iota((TL, C), 1), 1.0, 0.0).astype(BF16)
+    uv_rows = dot(pick, wuv[...]).astype(BF16)
+    for side in range(2):
+        for a in range(3):
+            source = iota((9 * C, TL), 0)
+            spread = jnp.where(source == (3 * a + 2 * side) * C + iota((9 * C, TL), 1) % C, 1.0, 0.0).astype(BF16)
+            side_mats[side, a] = jnp.where(sub // C == lane // C, dot(uv_rows, spread), 0.0).astype(BF16)
+
+    def spread_body(o, carry):
+        hit = (sub < 4 * C) & (sub % C == o) & (lane == jnp.where(sub < 2 * C, 0, TL - 1))
+        spread_mat[:, pl.ds(pl.multiple_of(o * TL, TL), TL)] = jnp.where(hit, 1.0, 0.0).astype(BF16)
+        return carry
+
+    lax.fori_loop(0, C, spread_body, 0)
 
     def wait_group(g, count):
         pltpu.make_async_remote_copy(
@@ -298,28 +327,37 @@
             value = jnp.where(lane == i, ref[index], value)
         return value
 
-    def mark_group(g, carry):
+    def mark_group(g):
         ids = jnp.concatenate([lanes_of(tiles, g, 0), lanes_of(tiles, g, 1)], axis=1)
         for m in range(4):
             hot = jnp.where(iota((256, 256), 0) + m * 256 == ids, 1.0, 0.0).astype(BF16)
-            onehot[g, m * 256 : (m + 1) * 256, :] = hot
-        return carry
+            onehot[m * 256 : (m + 1) * 256, :] = hot
 
     def weigh_group(g, carry):
+        mark_group(g)
         weights = jnp.concatenate([lanes_of(scale_in, g, 0), lanes_of(scale_in, g, 1)], axis=1)
         weights = jnp.broadcast_to(weights, (TL, 256)).astype(BF16)
         for m in range(4):
             at = slice(m * 256, (m + 1) * 256)
-            wsum[at, :] += lax.dot_general(onehot[g, at, :], weights, NT, preferred_element_type=F32)
+            wsum[at, :] += lax.dot_general(onehot[at, :], weights, NT, preferred_element_type=F32)
         return carry
 
     def group_sum(g, t, m):
         block = jnp.concatenate(
             [inbox[pl.ds(g * GROUP, GROUP), 2 * t + h].reshape(256, TL) for h in range(2)], axis=1
         )
-        return dot(onehot[g, m * 256 : (m + 1) * 256, :], block)
+        return dot(onehot[m * 256 : (m + 1) * 256, :], block)
+
+    def add_columns(g):
+        rows = [inbox[pl.ds(g * GROUP, GROUP), q].reshape(256, TL) for q in range(C)]
+        picked = dot(jnp.concatenate(rows, axis=1), pick_cols[...]).astype(BF16)
+        for m in range(4):
+            at = slice(m * 256, (m + 1) * 256)
+            col_sum[at, :] += dot(onehot[at, :], picked)
 
     def add_group(g):
+        add_columns(g)
+
         def channels(t, carry):
             for m in range(4):
                 got = group_sum(g, t, m)
@@ -330,11 +368,12 @@
 
         lax.fori_loop(0, C // 2, channels, 0)
 
-    lax.fori_loop(0, PEERS // GROUP, mark_group, 0)
+    mark_group(0)
     wait_group(0, GROUP - 1)
     add_group(0)
 
     def receive(g, carry):
+        mark_group(g)
         wait_group(g, GROUP)
         add_group(g)
         return carry
@@ -349,6 +388,39 @@
     wsum[...] = 1.0 / jnp.maximum(wsum[...], 1.0)
     wait_group(last, GROUP)
 
+    add_columns(last)
+
+    def collect(rb, carry):
+        at = pl.ds(pl.multiple_of(rb * TL, TL), TL)
+        values = [(col_sum[at, side * TL : (side + 1) * TL] * wsum[at, :]).astype(BF16).astype(F32) for side in range(2)]
+        return tuple(c + pltpu.roll(v, rb * C, 1) for c, v in zip(carry, values))
+
+    zero = jnp.zeros((TL, TL), F32)
+    left, right = lax.fori_loop(0, AR_DEV // TL, collect, (zero, zero))
+    cols[0] = left.astype(BF16)
+    cols[1] = right.astype(BF16)
+
+    west, east = lax.rem(cam + cams - 1, cams), lax.rem(cam + 1, cams)
+    north, south = lax.rem(row + strips - 1, strips), lax.rem(row + 1, strips)
+    plan = [
+        (cols.at[1], side_in.at[0], (east, row)),
+        (cols.at[0], side_in.at[1], (west, row)),
+        (cols.at[1, pl.ds(112, 16)], col_in.at[0], (east, south)),
+        (cols.at[1, pl.ds(0, 16)], col_in.at[1], (east, north)),
+        (cols.at[0, pl.ds(112, 16)], col_in.at[2], (west, south)),
+        (cols.at[0, pl.ds(0, 16)], col_in.at[3], (west, north)),
+        (above.at[64], row_in.at[0], (cam, south)),
+        (below.at[0], row_in.at[1], (cam, north)),
+    ]
+    copies = [
+        pltpu.make_async_remote_copy(
+            src_ref=src, dst_ref=dst, send_sem=hsend.at[i], recv_sem=hrecv.at[i], device_id=where, device_id_type=MESH
+        )
+        for i, (src, dst, where) in enumerate(plan)
+    ]
+    for copy in copies[:6]:
+        copy.start()
+
     def finish(t, carry):
         for m in range(4):
             got = group_sum(last, t, m)
@@ -373,128 +445,95 @@
 
     lax.fori_loop(0, 64, ends, 0)
 
-    def normal(rb, carry):
+    for copy in copies[6:]:
+        copy.start()
+    for copy in copies[:6]:
+        copy.wait()
+
+    has_side = ((cam > 0).astype(F32), (cam < cams - 1).astype(F32))
+    for side in range(2):
+        own = side_in[side].astype(F32) * has_side[side]
+        top = col_in[2 * side].astype(F32)[15:16, :] * (has_side[side] * has_above)
+        bottom = col_in[2 * side + 1].astype(F32)[0:1, :] * (has_side[side] * has_below)
+        before = jnp.where(lane[0:1] >= TL - C, top, own[TL - 1 : TL, :])
+        before = pltpu.roll(jnp.broadcast_to(before, (TL, TL)), C, 1)
+        after = jnp.where(lane[0:1] < C, bottom, own[0:1, :])
+        after = pltpu.roll(jnp.broadcast_to(after, (TL, TL)), TL - C, 1)
+        shifted = (
+            jnp.where(sub == 0, before, pltpu.roll(own, 1, 0)),
+            own,
+            jnp.where(sub == TL - 1, after, pltpu.roll(own, TL - 1, 0)),
+        )
+        result = jnp.zeros((TL, TL), F32)
+        for a in range(3):
+            result = result + lax.dot_general(
+                shifted[a].astype(BF16), side_mats[side, a], NT, preferred_element_type=F32
+            )
+        high = result.astype(BF16).astype(F32)
+        side_parts[2 * side] = high
+        side_parts[2 * side + 1] = result - high
+
+    tile_lane = iota((16, TL), 1)
+
+    def out_copy(rb):
         at = pl.ds(pl.multiple_of(rb * TL, TL), TL)
-        parts = [joined[q, at, :] for q in range(C)]
-        picked = dot(jnp.concatenate(parts, axis=1), pick_cols[...])
-        left = pltpu.roll(picked[:, :TL], rb * C, 1)
-        right = pltpu.roll(picked[:, TL:], rb * C, 1)
-        return carry[0] + left, carry[1] + right
-
-    zero = jnp.zeros((TL, TL), F32)
-    left, right = lax.fori_loop(0, AR_DEV // TL, normal, (zero, zero))
-    cols[0] = left.astype(BF16)
-    cols[1] = right.astype(BF16)
-
-    west, east = lax.rem(cam + cams - 1, cams), lax.rem(cam + 1, cams)
-    north, south = lax.rem(row + strips - 1, strips), lax.rem(row + 1, strips)
-    plan = [
-        (cols.at[1], side_in.at[0], (east, row)),
-        (cols.at[0], side_in.at[1], (west, row)),
-        (above.at[64], row_in.at[0], (cam, south)),
-        (below.at[0], row_in.at[1], (cam, north)),
-        (cols.at[1, pl.ds(112, 16)], col_in.at[0], (east, south)),
-        (cols.at[1, pl.ds(0, 16)], col_in.at[1], (east, north)),
-        (cols.at[0, pl.ds(112, 16)], col_in.at[2], (west, south)),
-        (cols.at[0, pl.ds(0, 16)], col_in.at[3], (west, north)),
-    ]
-    copies = [
-        pltpu.make_async_remote_copy(
-            src_ref=src, dst_ref=dst, send_sem=hsend.at[i], recv_sem=hrecv.at[i], device_id=where, device_id_type=MESH
-        )
-        for i, (src, dst, where) in enumerate(plan)
-    ]
-    for copy in copies:
-        copy.start()
+        return pltpu.make_async_copy(joined.at[:, at, :], texture.at[:, at, :], out_sem.at[rb])
+
+    def uv_block(rb, carry):
+        parts = zero
+        for k in range(4):
+            turned_part = pltpu.roll(side_parts[k], lax.rem(k * C + TL - rb * C, TL), 1)
+            parts = jnp.where(lane // C == k, turned_part, parts)
+        parts = parts.astype(BF16)
+        for n in range(4):
+            at = slice(n * 512, (n + 1) * 512)
+            part_a[0, 0:TL, at] = dot(parts, spread_mat[:, at])
+        for pair in range(4):
+            fields = []
+            for h in range(2):
+                g = pair * 2 + h
+                here = pl.ds(pl.multiple_of(rb * TL + g * 16, 16), 16)
+                fields.append(
+                    jnp.concatenate([joined[:, here, :].reshape(256, TL), above[rb * 8 + g], below[rb * 8 + g + 1]], axis=0)
+                )
+            taps = dot(band_uv[...], jnp.concatenate(fields, axis=1))
+            for h in range(2):
+                g = pair * 2 + h
+                here = pl.ds(pl.multiple_of(rb * TL + g * 16, 16), 16)
+                cut = slice(h * TL, (h + 1) * TL)
+                a = pltpu.roll(taps[0:256, cut], 1, 1)
+                m = taps[256:512, cut]
+                b = pltpu.roll(taps[512:768, cut], TL - 1, 1)
+                for o in range(C):
+                    rows = slice(o * 16, (o + 1) * 16)
+                    low = jnp.where(tile_lane == 0, 0.0, a[rows])
+                    high = jnp.where(tile_lane == TL - 1, 0.0, b[rows])
+                    side = part_a[0, g * 16 : (g + 1) * 16, o * TL : (o + 1) * TL]
+                    value = joined[o, here, :].astype(F32) + side + m[rows] + low + high
+                    joined[o, here, :] = value.astype(BF16)
+        out_copy(rb).start()
+        return carry
+
+    lax.fori_loop(1, 7, uv_block, 0)
     pltpu.make_async_remote_copy(
         src_ref=outbox.at[pl.ds(0, PEERS - 1)], dst_ref=inbox.at[pl.ds(0, PEERS - 1)], send_sem=send_sem,
         recv_sem=recv_sem.at[0], device_id=up, device_id_type=MESH,
     ).wait_send()
-    for copy in copies:
+    for copy in copies[6:]:
         copy.wait()
-    has_west = (cam > 0).astype(F32)
-    has_east = (cam < cams - 1).astype(F32)
-    side_cols[0] = side_in[0] * has_west.astype(BF16)
-    side_cols[1] = side_in[1] * has_east.astype(BF16)
     above[0] = row_in[0] * above_bf
     below[64] = row_in[1] * below_bf
-    for i, factor in enumerate(
-        (has_west * has_above, has_west * has_below, has_east * has_above, has_east * has_below)
-    ):
-        corners[i] = col_in[i] * factor.astype(BF16)
-
-
-def uv_kernel(weight, joined, above, below, side_cols, corners, texture, bands, delta):
-    rb = pl.program_id(0)
-
-    @pl.when(rb == 0)
-    def _():
-        def out_of(i):
-            return i // 16, i % 16
-
-        def in_of(i):
-            late = i - 256
-            return (
-                jnp.where(i < 256, i // 16, late % C),
-                jnp.where(i < 256, i % 16, jnp.where(late < C, -1, 16)),
-            )
-
-        for b, taps in enumerate(band(weight[...], 256, 288, out_of, in_of)):
-            bands[b * 256 : (b + 1) * 256, :] = taps
-
-        lane = iota((TL, TL), 1)
-        sub = iota((TL, TL), 0)
-        pick = jnp.where(iota((TL, C), 0) % C == iota((TL, C), 1), 1.0, 0.0).astype(BF16)
-        rows = dot(pick, weight[...]).astype(BF16)
-        for side in range(2):
-            own = side_cols[side].astype(F32)
-            top = corners[2 * side].astype(F32)[15:16, :]
-            bottom = corners[2 * side + 1].astype(F32)[0:1, :]
-            before = jnp.where(lane[0:1] >= TL - C, top, own[TL - 1 : TL, :])
-            before = pltpu.roll(jnp.broadcast_to(before, (TL, TL)), C, 1)
-            after = jnp.where(lane[0:1] < C, bottom, own[0:1, :])
-            after = pltpu.roll(jnp.broadcast_to(after, (TL, TL)), TL - C, 1)
-            shifted = (
-                jnp.where(sub == 0, before, pltpu.roll(own, 1, 0)),
-                own,
-                jnp.where(sub == TL - 1, after, pltpu.roll(own, TL - 1, 0)),
-            )
-            result = jnp.zeros((TL, TL), F32)
-            for a in range(3):
-                source = iota((9 * C, TL), 0)
-                spread = jnp.where(source == (3 * a + 2 * side) * C + iota((9 * C, TL), 1) % C, 1.0, 0.0).astype(BF16)
-                matrix = jnp.where(sub // C == lane // C, dot(rows, spread), 0.0).astype(BF16)
-                result = result + lax.dot_general(shifted[a].astype(BF16), matrix, NT, preferred_element_type=F32)
-            delta[side] = result
-
-    turn = lax.rem(TL - rb * C, TL)
-    left = pltpu.roll(delta[0], turn, 1)
-    right = pltpu.roll(delta[1], turn, 1)
-    lane = iota((16, TL), 1)
-    for pair in range(4):
-        fields = []
-        for h in range(2):
-            g = pair * 2 + h
-            at = rb * 8 + g
-            fields.append(
-                jnp.concatenate(
-                    [joined[:, g * 16 : (g + 1) * 16, :].reshape(256, TL), above[at], below[at + 1]], axis=0
-                )
-            )
-        taps = dot(bands[...], jnp.concatenate(fields, axis=1))
-        for h in range(2):
-            g = pair * 2 + h
-            cut = slice(h * TL, (h + 1) * TL)
-            a = pltpu.roll(taps[0:256, cut], 1, 1)
-            m = taps[256:512, cut]
-            b = pltpu.roll(taps[512:768, cut], TL - 1, 1)
-            for o in range(C):
-                rows = slice(o * 16, (o + 1) * 16)
-                here = slice(g * 16, (g + 1) * 16)
-                low = jnp.where(lane == 0, left[here, o : o + 1], a[rows])
-                high = jnp.where(lane == TL - 1, right[here, o : o + 1], b[rows])
-                value = joined[o, here, :].astype(F32) + m[rows] + low + high
-                texture[o, here, :] = value.astype(BF16)
+
+    def outer_block(i, carry):
+        return uv_block(i * 7, carry)
+
+    lax.fori_loop(0, 2, outer_block, 0)
+
+    def out_wait(rb, carry):
+        out_copy(rb).wait()
+        return carry
+
+    lax.fori_loop(0, 8, out_wait, 0)
 
 
 def local(image, conv_first, conv_second, conv_uv, send_block, send_shift, send_weight, send_count, recv_tile):
@@ -510,18 +549,20 @@
     vmem = pl.BlockSpec(memory_space=pltpu.VMEM)
     smem = pl.BlockSpec(memory_space=pltpu.SMEM)
     dma = pltpu.SemaphoreType.DMA
-    joined, above, below, side_cols, corners = pl.pallas_call(
+    return pl.pallas_call(
         join_kernel,
-        out_shape=[
-            jax.ShapeDtypeStruct((C, AR_DEV, TL), BF16),
-            jax.ShapeDtypeStruct((65, C, TL), BF16),
-            jax.ShapeDtypeStruct((65, C, TL), BF16),
-            jax.ShapeDtypeStruct((2, TL, TL), BF16),
-            jax.ShapeDtypeStruct((4, 16, TL), BF16),
-        ],
-        in_specs=[vmem, vmem, vmem, smem, vmem, vmem],
-        out_specs=[vmem] * 5,
+        out_shape=jax.ShapeDtypeStruct((C, AR_DEV, TL), BF16),
+        in_specs=[vmem, vmem, vmem, vmem, smem, vmem, vmem],
+        out_specs=pl.BlockSpec(memory_space=pl.ANY),
         scratch_shapes=[
+            pltpu.VMEM((C, AR_DEV, TL), BF16),
+            pltpu.VMEM((65, C, TL), BF16),
+            pltpu.VMEM((65, C, TL), BF16),
+            pltpu.VMEM((768, 288), BF16),
+            pltpu.VMEM((2, 3, TL, TL), BF16),
+            pltpu.VMEM((TL, C * TL), BF16),
+            pltpu.VMEM((4, TL, TL), F32),
+            pltpu.VMEM((AR_DEV, 256), F32),
             pltpu.VMEM((3, 288, 256), BF16),
             pltpu.VMEM((2, 3, 32, 32), BF16),
             pltpu.VMEM((3, 224, 256), BF16),
@@ -536,7 +577,7 @@
             pltpu.VMEM((PEERS, C, CAP, TL), BF16),
             pltpu.VMEM((PEERS, C, CAP, TL), BF16),
             pltpu.VMEM((PEERS, 1, TL), F32),
-            pltpu.VMEM((PEERS // GROUP, AR_DEV, 256), BF16),
+            pltpu.VMEM((AR_DEV, 256), BF16),
             pltpu.VMEM((C * AR_DEV, TL), F32),
             pltpu.VMEM((AR_DEV, TL), F32),
             pltpu.VMEM((C * TL, 256), BF16),
@@ -544,32 +585,13 @@
             pltpu.VMEM((2, TL, TL), BF16),
             pltpu.VMEM((4, 16, TL), BF16),
             pltpu.VMEM((2, C, TL), BF16),
-            dma((2,)), dma((2,)), dma, dma((PEERS // GROUP,)), dma, dma, dma((8,)), dma((8,)),
+            dma((2,)), dma((2,)), dma, dma((PEERS // GROUP,)), dma, dma, dma((8,)), dma((8,)), dma((8,)),
         ],
         compiler_params=pltpu.CompilerParams(
             collective_id=0, has_side_effects=True, vmem_limit_bytes=62 * 1024 * 1024
         ),
         cost_estimate=pl.CostEstimate(flops=2 * 10**10, bytes_accessed=3 * 10**7, transcendentals=10**6),
-    )(image.reshape(C, ROWS, W), conv_first, conv_second, code, scale_rows, tiles)
-
-    full = lambda shape: pl.BlockSpec(shape, lambda i: (0,) * len(shape))
-    return pl.pallas_call(
-        uv_kernel,
-        out_shape=jax.ShapeDtypeStruct((C, AR_DEV, TL), BF16),
-        grid=(AR_DEV // TL,),
-        in_specs=[
-            full((C, 9 * C)),
-            pl.BlockSpec((C, TL, TL), lambda i: (0, i, 0)),
-            full((65, C, TL)),
-            full((65, C, TL)),
-            full((2, TL, TL)),
-            full((4, 16, TL)),
-        ],
-        out_specs=pl.BlockSpec((C, TL, TL), lambda i: (0, i, 0)),
-        scratch_shapes=[pltpu.VMEM((768, 288), BF16), pltpu.VMEM((2, TL, TL), F32)],
-        compiler_params=pltpu.CompilerParams(vmem_limit_bytes=62 * 1024 * 1024),
-        cost_estimate=pl.CostEstimate(flops=10**10, bytes_accessed=10**7, transcendentals=0),
-    )(conv_uv, joined, above, below, side_cols, corners)
+    )(image.reshape(C, ROWS, W), conv_first, conv_second, conv_uv, code, scale_rows, tiles)
 
 
 def solution(mesh):

time: 174 us -> 188 us (1.080)
  Pallas kernels: 165 us -> 176 us
  local copies, waits for them, and re-layouts: 3.44 us -> 8.06 us
    pallas_call x2 -> x1, Pallas kernels: 165 us -> 176 us  [local(): pl.pallas_call(join_kernel, out_shape=jax.ShapeDtypeStruct((C, AR_DEV, TL...]
    unnamed x1 -> x2, local copies, waits for them, and re-layouts: 0.79 us -> 5.4 us
where the time goes in v3:
time: 188 us; the launch traced here: 187 us
  Pallas kernels  176 us (94%)
  local copies, waits for them, and re-layouts  8.06 us (4%)
  other arithmetic  2.68 us (1%)
    pallas_call x1, Pallas kernels, local(): pl.pallas_call(join_kernel, out_shape=jax.ShapeDtypeStruct((C, AR_DEV, TL...  176 us
    unnamed x2, local copies, waits for them, and re-layouts  5.4 us

profile of v3, /device:TPU:1, one launch (start us, length us, event | category | flops | bytes accessed | tf_op | source)
XLA Modules:
  0.0 186.6 jit_solution(7983099602484467266)
XLA Ops:
  0.0 0.7 iota_compare_fusion
  0.7 0.7 multiply_add_fusion.1
  1.4 0.7 fusion.1
  2.1 0.1 copy.13
  2.2 0.1 lt.21
  2.3 0.7 copy.15.scale_rows
  3.1 0.1 copy.12
  3.2 0.1 add.12
  3.2 0.7 tile.20
  3.9 0.7 copy.16.tiles
  4.7 0.8 copy.14
  5.5 0.1 reshape.58
  5.6 0.6 multiply_add_fusion.code
  6.2 175.9 %shard_map.91 = bf16[16,1024,128]{2,1,0:T(8,128)(2,1)} custom-call(bf16[16,32,2048]{2,1,0:T(8,128)(2,1)} %bitcast.20, bf16[16,144]{1,0:T(8,128)(2,1)} %w1.1, bf16[16,144]{1,0:T(8,128)(2,1)} %w2.1, bf16[16,144]{1,0:T(8,128)(2,1)} %wuv.1, s32[2048]{0:T(1024)} %multiply_add_fusion.code, f32[128,1,128]{2,1,0:T(1,128)} %copy.15.scale_rows, s32[128,1,128]{2,1,0:T(1,128)} %copy.16.tiles), custom_call_target="tpu_custom_call" | custom-call | flops 20000000000 | bytes 30000000 | tf_op jit(solution)/shard_map/pallas_call | solution.py:552
  182.0 4.6 %copy.18 = bf16[16,1024,128]{2,1,0:T(8,128)(2,1)} copy(bf16[16,1024,128]{2,1,0:T(8,128)(2,1)} %shard_map.91) | data formatting | bytes 8388608
  (1 shorter events, 0.0 us)

commit v4 on v3

--- a/solution.py
+++ b/solution.py
@@ -2,6 +2,7 @@
 
 import jax
 import jax.numpy as jnp
+import numpy as np
 from jax import lax
 from jax.experimental import pallas as pl
 from jax.experimental.pallas import tpu as pltpu
@@ -19,6 +20,7 @@
 BF16 = jnp.bfloat16
 MESH = pl.DeviceIdType.MESH
 NT = (((1,), (1,)), ((), ()))
+TN = (((0,), (0,)), ((), ()))
 
 
 def iota(shape, dim):
@@ -62,9 +64,9 @@
 
 
 def join_kernel(
-    image, w1, w2, wuv, code, scale_rows, tiles,
-    texture,
-    joined, above, below, band_uv, side_mats, spread_mat, side_parts, col_sum,
+    image, w1, w2, wuv, code, code_rows, tile_rows,
+    joined_out, above, below, band_uv, side_parts,
+    joined, scale_rows, tiles, side_mats, col_sum,
     band1, band1h, band2, part_a, part_b, part_g, hidden, feats,
     edge_out, edge_in, turned, outbox, inbox, scale_in, onehot, total, wsum, pick_cols, cols, side_in, col_in, row_in,
     edge_send, edge_recv, send_sem, recv_sem, ssend_sem, srecv_sem, hsend, hrecv, out_sem,
@@ -83,6 +85,17 @@
         return carry
 
     lax.fori_loop(1, PEERS, greet, 0)
+
+    repeat = jnp.where(iota((CAP, TL), 1) % CAP == iota((CAP, TL), 0), 1.0, 0.0).astype(BF16)
+    def table(numbers):
+        return lax.dot_general(numbers.astype(F32).astype(BF16), repeat, TN, preferred_element_type=F32)
+
+    scale_table = table(code_rows[...] >> 16) * 0.0625
+    tile_table = table(tile_rows[...] >> 5) * 32.0 + table(tile_rows[...] & 31)
+    for i in range(PEERS // 8):
+        at = slice(i * 8, i * 8 + 8)
+        scale_rows[at] = scale_table[at].reshape(8, 1, TL)
+        tiles[at] = tile_table[at].reshape(8, 1, TL)
 
     def edges(n, carry):
         at = pl.ds(pl.multiple_of(n * 256, 256), 256)
@@ -229,7 +242,7 @@
 
     def make(p, slot, put_tile):
         for e in range(CAP):
-            word = code[p * CAP + e]
+            word = code[e, p]
             block = word & 511
             shift = (word >> 9) & 127
             scale = (word >> 16).astype(F32) * 0.0625
@@ -305,13 +318,6 @@
             spread = jnp.where(source == (3 * a + 2 * side) * C + iota((9 * C, TL), 1) % C, 1.0, 0.0).astype(BF16)
             side_mats[side, a] = jnp.where(sub // C == lane // C, dot(uv_rows, spread), 0.0).astype(BF16)
 
-    def spread_body(o, carry):
-        hit = (sub < 4 * C) & (sub % C == o) & (lane == jnp.where(sub < 2 * C, 0, TL - 1))
-        spread_mat[:, pl.ds(pl.multiple_of(o * TL, TL), TL)] = jnp.where(hit, 1.0, 0.0).astype(BF16)
-        return carry
-
-    lax.fori_loop(0, C, spread_body, 0)
-
     def wait_group(g, count):
         pltpu.make_async_remote_copy(
             src_ref=outbox.at[pl.ds(0, count)], dst_ref=inbox.at[pl.ds(0, count)], send_sem=send_sem,
@@ -330,7 +336,7 @@
     def mark_group(g):
         ids = jnp.concatenate([lanes_of(tiles, g, 0), lanes_of(tiles, g, 1)], axis=1)
         for m in range(4):
-            hot = jnp.where(iota((256, 256), 0) + m * 256 == ids, 1.0, 0.0).astype(BF16)
+            hot = jnp.where((iota((256, 256), 0) + m * 256).astype(F32) == ids, 1.0, 0.0).astype(BF16)
             onehot[m * 256 : (m + 1) * 256, :] = hot
 
     def weigh_group(g, carry):
@@ -421,6 +427,10 @@
     for copy in copies[:6]:
         copy.start()
 
+    def out_copy(t):
+        at = pl.ds(2 * t, 2)
+        return pltpu.make_async_copy(joined.at[at], joined_out.at[at], out_sem.at[t])
+
     def finish(t, carry):
         for m in range(4):
             got = group_sum(last, t, m)
@@ -429,6 +439,7 @@
                 value = (total[at, :] + got[:, h * TL : (h + 1) * TL]) * wsum[m * 256 : (m + 1) * 256, :]
                 total[at, :] = value
                 joined[2 * t + h, m * 256 : (m + 1) * 256, :] = value.astype(BF16)
+        out_copy(t).start()
         return carry
 
     lax.fori_loop(0, C // 2, finish, 0)
@@ -469,52 +480,10 @@
             result = result + lax.dot_general(
                 shifted[a].astype(BF16), side_mats[side, a], NT, preferred_element_type=F32
             )
-        high = result.astype(BF16).astype(F32)
+        high = result.astype(BF16)
         side_parts[2 * side] = high
-        side_parts[2 * side + 1] = result - high
-
-    tile_lane = iota((16, TL), 1)
-
-    def out_copy(rb):
-        at = pl.ds(pl.multiple_of(rb * TL, TL), TL)
-        return pltpu.make_async_copy(joined.at[:, at, :], texture.at[:, at, :], out_sem.at[rb])
-
-    def uv_block(rb, carry):
-        parts = zero
-        for k in range(4):
-            turned_part = pltpu.roll(side_parts[k], lax.rem(k * C + TL - rb * C, TL), 1)
-            parts = jnp.where(lane // C == k, turned_part, parts)
-        parts = parts.astype(BF16)
-        for n in range(4):
-            at = slice(n * 512, (n + 1) * 512)
-            part_a[0, 0:TL, at] = dot(parts, spread_mat[:, at])
-        for pair in range(4):
-            fields = []
-            for h in range(2):
-                g = pair * 2 + h
-                here = pl.ds(pl.multiple_of(rb * TL + g * 16, 16), 16)
-                fields.append(
-                    jnp.concatenate([joined[:, here, :].reshape(256, TL), above[rb * 8 + g], below[rb * 8 + g + 1]], axis=0)
-                )
-            taps = dot(band_uv[...], jnp.concatenate(fields, axis=1))
-            for h in range(2):
-                g = pair * 2 + h
-                here = pl.ds(pl.multiple_of(rb * TL + g * 16, 16), 16)
-                cut = slice(h * TL, (h + 1) * TL)
-                a = pltpu.roll(taps[0:256, cut], 1, 1)
-                m = taps[256:512, cut]
-                b = pltpu.roll(taps[512:768, cut], TL - 1, 1)
-                for o in range(C):
-                    rows = slice(o * 16, (o + 1) * 16)
-                    low = jnp.where(tile_lane == 0, 0.0, a[rows])
-                    high = jnp.where(tile_lane == TL - 1, 0.0, b[rows])
-                    side = part_a[0, g * 16 : (g + 1) * 16, o * TL : (o + 1) * TL]
-                    value = joined[o, here, :].astype(F32) + side + m[rows] + low + high
-                    joined[o, here, :] = value.astype(BF16)
-        out_copy(rb).start()
-        return carry
-
-    lax.fori_loop(1, 7, uv_block, 0)
+        side_parts[2 * side + 1] = (result - high.astype(F32)).astype(BF16)
+
     pltpu.make_async_remote_copy(
         src_ref=outbox.at[pl.ds(0, PEERS - 1)], dst_ref=inbox.at[pl.ds(0, PEERS - 1)], send_sem=send_sem,
         recv_sem=recv_sem.at[0], device_id=up, device_id_type=MESH,
@@ -524,44 +493,75 @@
     above[0] = row_in[0] * above_bf
     below[64] = row_in[1] * below_bf
 
-    def outer_block(i, carry):
-        return uv_block(i * 7, carry)
-
-    lax.fori_loop(0, 2, outer_block, 0)
-
-    def out_wait(rb, carry):
-        out_copy(rb).wait()
-        return carry
-
-    lax.fori_loop(0, 8, out_wait, 0)
+    def out_wait(t, carry):
+        out_copy(t).wait()
+        return carry
+
+    lax.fori_loop(0, C // 2, out_wait, 0)
+
+
+def uv_kernel(joined, above, below, bands, side_parts, spread_mat, texture, side_plane):
+    rb = pl.program_id(0)
+    lane = iota((TL, TL), 1)
+    parts = jnp.zeros((TL, TL), F32)
+    for k in range(4):
+        turned = pltpu.roll(side_parts[k].astype(F32), lax.rem(k * C + TL - rb * C, TL), 1)
+        parts = jnp.where(lane // C == k, turned, parts)
+    parts = parts.astype(BF16)
+    for n in range(4):
+        at = slice(n * 512, (n + 1) * 512)
+        side_plane[:, at] = dot(parts, spread_mat[:, at])
+    tile_lane = iota((16, TL), 1)
+    for pair in range(4):
+        fields = []
+        for h in range(2):
+            g = pair * 2 + h
+            here = slice(g * 16, (g + 1) * 16)
+            fields.append(
+                jnp.concatenate([joined[:, here, :].reshape(256, TL), above[rb * 8 + g], below[rb * 8 + g + 1]], axis=0)
+            )
+        taps = dot(bands[...], jnp.concatenate(fields, axis=1))
+        for h in range(2):
+            g = pair * 2 + h
+            here = slice(g * 16, (g + 1) * 16)
+            cut = slice(h * TL, (h + 1) * TL)
+            a = pltpu.roll(taps[0:256, cut], 1, 1)
+            m = taps[256:512, cut]
+            b = pltpu.roll(taps[512:768, cut], TL - 1, 1)
+            for o in range(C):
+                rows = slice(o * 16, (o + 1) * 16)
+                low = jnp.where(tile_lane == 0, 0.0, a[rows])
+                high = jnp.where(tile_lane == TL - 1, 0.0, b[rows])
+                side = side_plane[here, o * TL : (o + 1) * TL]
+                value = joined[o, here, :].astype(F32) + side + m[rows] + low + high
+                texture[o, here, :] = value.astype(BF16)
 
 
 def local(image, conv_first, conv_second, conv_uv, send_block, send_shift, send_weight, send_count, recv_tile):
-    block = send_block.reshape(PEERS, CAP)
-    shift = send_shift.reshape(PEERS, CAP)
-    valid = lax.broadcasted_iota(jnp.int32, (PEERS, CAP), 1) < send_count.reshape(PEERS, 1)
-    weight = jnp.where(valid, send_weight.reshape(PEERS, CAP), 0)
-    code = (block + shift * 512 + weight * 65536).reshape(PEERS * CAP)
-    scale = weight.astype(F32) * 0.0625
-    scale_rows = jnp.tile(scale, (1, 8)).reshape(PEERS, 1, TL)
-    tiles = jnp.tile(recv_tile.reshape(PEERS, CAP), (1, 8)).reshape(PEERS, 1, TL)
+    valid = lax.broadcasted_iota(jnp.int32, (CAP, PEERS), 0) < send_count.reshape(1, PEERS)
+    weight = jnp.where(valid, send_weight.reshape(PEERS, CAP).T, 0)
+    code = send_block.reshape(PEERS, CAP).T + send_shift.reshape(PEERS, CAP).T * 512 + weight * 65536
+    tile_rows = recv_tile.reshape(PEERS, CAP).T
 
     vmem = pl.BlockSpec(memory_space=pltpu.VMEM)
     smem = pl.BlockSpec(memory_space=pltpu.SMEM)
     dma = pltpu.SemaphoreType.DMA
-    return pl.pallas_call(
+    joined, above, below, bands, side_parts = pl.pallas_call(
         join_kernel,
-        out_shape=jax.ShapeDtypeStruct((C, AR_DEV, TL), BF16),
+        out_shape=[
+            jax.ShapeDtypeStruct((C, AR_DEV, TL), BF16),
+            jax.ShapeDtypeStruct((65, C, TL), BF16),
+            jax.ShapeDtypeStruct((65, C, TL), BF16),
+            jax.ShapeDtypeStruct((768, 288), BF16),
+            jax.ShapeDtypeStruct((4, TL, TL), BF16),
+        ],
         in_specs=[vmem, vmem, vmem, vmem, smem, vmem, vmem],
-        out_specs=pl.BlockSpec(memory_space=pl.ANY),
+        out_specs=[pl.BlockSpec(memory_space=pl.ANY)] + [vmem] * 4,
         scratch_shapes=[
             pltpu.VMEM((C, AR_DEV, TL), BF16),
-            pltpu.VMEM((65, C, TL), BF16),
-            pltpu.VMEM((65, C, TL), BF16),
-            pltpu.VMEM((768, 288), BF16),
+            pltpu.VMEM((PEERS, 1, TL), F32),
+            pltpu.VMEM((PEERS, 1, TL), F32),
             pltpu.VMEM((2, 3, TL, TL), BF16),
-            pltpu.VMEM((TL, C * TL), BF16),
-            pltpu.VMEM((4, TL, TL), F32),
             pltpu.VMEM((AR_DEV, 256), F32),
             pltpu.VMEM((3, 288, 256), BF16),
             pltpu.VMEM((2, 3, 32, 32), BF16),
@@ -591,7 +591,29 @@
             collective_id=0, has_side_effects=True, vmem_limit_bytes=62 * 1024 * 1024
         ),
         cost_estimate=pl.CostEstimate(flops=2 * 10**10, bytes_accessed=3 * 10**7, transcendentals=10**6),
-    )(image.reshape(C, ROWS, W), conv_first, conv_second, conv_uv, code, scale_rows, tiles)
+    )(image.reshape(C, ROWS, W), conv_first, conv_second, conv_uv, code, code, tile_rows)
+
+    k, o = np.arange(TL)[:, None, None] // C, np.arange(TL)[:, None, None] % C
+    channel, column = np.arange(C)[None, :, None], np.arange(TL)[None, None, :]
+    spread = ((k < 4) & (o == channel) & (column == np.where(k < 2, 0, TL - 1))).reshape(TL, C * TL)
+    full = lambda shape: pl.BlockSpec(shape, lambda i: (0,) * len(shape))
+    return pl.pallas_call(
+        uv_kernel,
+        out_shape=jax.ShapeDtypeStruct((C, AR_DEV, TL), BF16),
+        grid=(AR_DEV // TL,),
+        in_specs=[
+            pl.BlockSpec((C, TL, TL), lambda i: (0, i, 0)),
+            full((65, C, TL)),
+            full((65, C, TL)),
+            full((768, 288)),
+            full((4, TL, TL)),
+            full((TL, C * TL)),
+        ],
+        out_specs=pl.BlockSpec((C, TL, TL), lambda i: (0, i, 0)),
+        scratch_shapes=[pltpu.VMEM((TL, C * TL), F32)],
+        compiler_params=pltpu.CompilerParams(vmem_limit_bytes=62 * 1024 * 1024),
+        cost_estimate=pl.CostEstimate(flops=10**10, bytes_accessed=10**7, transcendentals=0),
+    )(joined, above, below, bands, side_parts, jnp.asarray(spread.astype(np.float32)).astype(BF16))
 
 
 def solution(mesh):

time: 188 us -> 171 us (0.910)
  local copies, waits for them, and re-layouts: 8.06 us -> 0 us
  Pallas kernels: 176 us -> 169 us
    pallas_call x1 -> x2, Pallas kernels: 176 us -> 169 us  [the longest x1 156 us: local(): pl.pallas_call(join_kernel, out_shape=[jax.ShapeDtypeStruct((C, AR_DEV, T...]
    unnamed x2 -> x0, local copies, waits for them, and re-layouts: 5.4 us -> none
    another operation x4 -> x0, local copies, waits for them, and re-layouts: 2.18 us -> none  [the longest x2 1.44 us: local(): jnp.tile(recv_tile.reshape(PEERS, CAP), (1, 8)).reshape(PEERS, 1, TL)]
where the time goes in v4:
time: 171 us; the launch traced here: 170 us
  Pallas kernels  169 us (99%)
    pallas_call x1, Pallas kernels, local(): pl.pallas_call(join_kernel, out_shape=[jax.ShapeDtypeStruct((C, AR_DEV, T...  156 us
    pallas_call x1, Pallas kernels, local(): pl.pallas_call(uv_kernel, out_shape=jax.ShapeDtypeStruct((C, AR_DEV, TL),...  13.2 us

profile of v4, /device:TPU:1, one launch (start us, length us, event | category | flops | bytes accessed | tf_op | source)
XLA Modules:
  0.0 170.4 jit_solution(2960311840960958447)
XLA Ops:
  0.0 1.3 fusion.1.code.code_rows
  1.3 155.8 %shard_map.100 = (bf16[16,1024,128]{2,1,0:T(8,128)(2,1)}, bf16[65,16,128]{2,1,0:T(8,128)(2,1)}, bf16[65,16,128]{2,1,0:T(8,128)(2,1)}, bf16[768,288]{1,0:T(8,128)(2,1)}, bf16[4,128,128]{2,1,0:T(8,128)(2,1)}) custom-call(bf16[16,32,2048]{2,1,0:T(8,128)(2,1)} %bitcast.18, bf16[16,144]{1,0:T(8,128)(2,1)} %w1.1, bf16[16,144]{1,0:T(8,128)(2,1)} %w2.1, ...), custom_call_target="tpu_custom_call" | custom-call | flops 20000000000 | bytes 30000000 | tf_op jit(solution)/shard_map/pallas_call | solution.py:549
  157.2 13.2 %shard_map.101 = bf16[16,1024,128]{2,1,0:T(8,128)(2,1)} custom-call(bf16[16,1024,128]{2,1,0:T(8,128)(2,1)} %get-tuple-element.10.joined, bf16[65,16,128]{2,1,0:T(8,128)(2,1)} %get-tuple-element.11.above, bf16[65,16,128]{2,1,0:T(8,128)(2,1)} %get-tuple-element.12.below, bf16[768,288]{1,0:T(8,128)(2,1)} %get-tuple-element.13.bands, ...), custom_call_target="tpu_custom_call" | custom-call | flops 10000000000 | bytes 10000000 | tf_op jit(solution)/shard_map/pallas_call | solution.py:600

commit v5 on v4

--- a/solution.py
+++ b/solution.py
@@ -352,7 +352,7 @@
         block = jnp.concatenate(
             [inbox[pl.ds(g * GROUP, GROUP), 2 * t + h].reshape(256, TL) for h in range(2)], axis=1
         )
-        return dot(onehot[m * 256 : (m + 1) * 256, :], block)
+        return dot(onehot[m * 1024 : (m + 1) * 1024, :], block)
 
     def add_columns(g):
         rows = [inbox[pl.ds(g * GROUP, GROUP), q].reshape(256, TL) for q in range(C)]
@@ -365,10 +365,10 @@
         add_columns(g)
 
         def channels(t, carry):
-            for m in range(4):
+            for m in range(1):
                 got = group_sum(g, t, m)
                 for h in range(2):
-                    at = pl.ds(pl.multiple_of((2 * t + h) * AR_DEV + m * 256, 256), 256)
+                    at = pl.ds(pl.multiple_of((2 * t + h) * AR_DEV + m * 1024, 1024), 1024)
                     total[at, :] += got[:, h * TL : (h + 1) * TL]
             return carry
 
@@ -432,13 +432,13 @@
         return pltpu.make_async_copy(joined.at[at], joined_out.at[at], out_sem.at[t])
 
     def finish(t, carry):
-        for m in range(4):
+        for m in range(1):
             got = group_sum(last, t, m)
             for h in range(2):
-                at = pl.ds(pl.multiple_of((2 * t + h) * AR_DEV + m * 256, 256), 256)
-                value = (total[at, :] + got[:, h * TL : (h + 1) * TL]) * wsum[m * 256 : (m + 1) * 256, :]
+                at = pl.ds(pl.multiple_of((2 * t + h) * AR_DEV + m * 1024, 1024), 1024)
+                value = (total[at, :] + got[:, h * TL : (h + 1) * TL]) * wsum[m * 1024 : (m + 1) * 1024, :]
                 total[at, :] = value
-                joined[2 * t + h, m * 256 : (m + 1) * 256, :] = value.astype(BF16)
+                joined[2 * t + h, m * 1024 : (m + 1) * 1024, :] = value.astype(BF16)
         out_copy(t).start()
         return carry
 
@@ -501,40 +501,41 @@
 
 
 def uv_kernel(joined, above, below, bands, side_parts, spread_mat, texture, side_plane):
-    rb = pl.program_id(0)
-    lane = iota((TL, TL), 1)
-    parts = jnp.zeros((TL, TL), F32)
-    for k in range(4):
-        turned = pltpu.roll(side_parts[k].astype(F32), lax.rem(k * C + TL - rb * C, TL), 1)
-        parts = jnp.where(lane // C == k, turned, parts)
-    parts = parts.astype(BF16)
-    for n in range(4):
-        at = slice(n * 512, (n + 1) * 512)
-        side_plane[:, at] = dot(parts, spread_mat[:, at])
-    tile_lane = iota((16, TL), 1)
-    for pair in range(4):
-        fields = []
-        for h in range(2):
-            g = pair * 2 + h
-            here = slice(g * 16, (g + 1) * 16)
-            fields.append(
-                jnp.concatenate([joined[:, here, :].reshape(256, TL), above[rb * 8 + g], below[rb * 8 + g + 1]], axis=0)
-            )
-        taps = dot(bands[...], jnp.concatenate(fields, axis=1))
-        for h in range(2):
-            g = pair * 2 + h
-            here = slice(g * 16, (g + 1) * 16)
-            cut = slice(h * TL, (h + 1) * TL)
-            a = pltpu.roll(taps[0:256, cut], 1, 1)
-            m = taps[256:512, cut]
-            b = pltpu.roll(taps[512:768, cut], TL - 1, 1)
-            for o in range(C):
-                rows = slice(o * 16, (o + 1) * 16)
-                low = jnp.where(tile_lane == 0, 0.0, a[rows])
-                high = jnp.where(tile_lane == TL - 1, 0.0, b[rows])
-                side = side_plane[here, o * TL : (o + 1) * TL]
-                value = joined[o, here, :].astype(F32) + side + m[rows] + low + high
-                texture[o, here, :] = value.astype(BF16)
+    for half in range(2):
+        rb = pl.program_id(0) * 2 + half
+        lane = iota((TL, TL), 1)
+        parts = jnp.zeros((TL, TL), F32)
+        for k in range(4):
+            turned = pltpu.roll(side_parts[k].astype(F32), lax.rem(k * C + TL - rb * C, TL), 1)
+            parts = jnp.where(lane // C == k, turned, parts)
+        parts = parts.astype(BF16)
+        for n in range(4):
+            at = slice(n * 512, (n + 1) * 512)
+            side_plane[:, at] = dot(parts, spread_mat[:, at])
+        tile_lane = iota((16, TL), 1)
+        for pair in range(4):
+            fields = []
+            for h in range(2):
+                g = pair * 2 + h
+                here = slice(half * TL + g * 16, half * TL + (g + 1) * 16)
+                fields.append(
+                    jnp.concatenate([joined[:, here, :].reshape(256, TL), above[rb * 8 + g], below[rb * 8 + g + 1]], axis=0)
+                )
+            taps = dot(bands[...], jnp.concatenate(fields, axis=1))
+            for h in range(2):
+                g = pair * 2 + h
+                here = slice(half * TL + g * 16, half * TL + (g + 1) * 16)
+                cut = slice(h * TL, (h + 1) * TL)
+                a = pltpu.roll(taps[0:256, cut], 1, 1)
+                m = taps[256:512, cut]
+                b = pltpu.roll(taps[512:768, cut], TL - 1, 1)
+                for o in range(C):
+                    rows = slice(o * 16, (o + 1) * 16)
+                    low = jnp.where(tile_lane == 0, 0.0, a[rows])
+                    high = jnp.where(tile_lane == TL - 1, 0.0, b[rows])
+                    side = side_plane[g * 16 : (g + 1) * 16, o * TL : (o + 1) * TL]
+                    value = joined[o, here, :].astype(F32) + side + m[rows] + low + high
+                    texture[o, here, :] = value.astype(BF16)
 
 
 def local(image, conv_first, conv_second, conv_uv, send_block, send_shift, send_weight, send_count, recv_tile):
@@ -600,16 +601,16 @@
     return pl.pallas_call(
         uv_kernel,
         out_shape=jax.ShapeDtypeStruct((C, AR_DEV, TL), BF16),
-        grid=(AR_DEV // TL,),
+        grid=(AR_DEV // TL // 2,),
         in_specs=[
-            pl.BlockSpec((C, TL, TL), lambda i: (0, i, 0)),
+            pl.BlockSpec((C, 2 * TL, TL), lambda i: (0, i, 0)),
             full((65, C, TL)),
             full((65, C, TL)),
             full((768, 288)),
             full((4, TL, TL)),
             full((TL, C * TL)),
         ],
-        out_specs=pl.BlockSpec((C, TL, TL), lambda i: (0, i, 0)),
+        out_specs=pl.BlockSpec((C, 2 * TL, TL), lambda i: (0, i, 0)),
         scratch_shapes=[pltpu.VMEM((TL, C * TL), F32)],
         compiler_params=pltpu.CompilerParams(vmem_limit_bytes=62 * 1024 * 1024),
         cost_estimate=pl.CostEstimate(flops=10**10, bytes_accessed=10**7, transcendentals=0),

time: 171 us -> 169 us (0.988)
  no operation moved by 1% of the time
where the time goes in v5:
time: 169 us
  Pallas kernels  168 us (99%)
    pallas_call x1, Pallas kernels, local(): pl.pallas_call(join_kernel, out_shape=[jax.ShapeDtypeStruct((C, AR_DEV, T...  156 us
    pallas_call x1, Pallas kernels, local(): pl.pallas_call(uv_kernel, out_shape=jax.ShapeDtypeStruct((C, AR_DEV, TL),...  12 us

profile of v5, /device:TPU:1, one launch (start us, length us, event | category | flops | bytes accessed | tf_op | source)
XLA Modules:
  0.0 169.0 jit_solution(14741146099320685614)
XLA Ops:
  0.0 1.3 fusion.1.code.code_rows
  1.3 155.7 %shard_map.100 = (bf16[16,1024,128]{2,1,0:T(8,128)(2,1)}, bf16[65,16,128]{2,1,0:T(8,128)(2,1)}, bf16[65,16,128]{2,1,0:T(8,128)(2,1)}, bf16[768,288]{1,0:T(8,128)(2,1)}, bf16[4,128,128]{2,1,0:T(8,128)(2,1)}) custom-call(bf16[16,32,2048]{2,1,0:T(8,128)(2,1)} %bitcast.18, bf16[16,144]{1,0:T(8,128)(2,1)} %w1.1, bf16[16,144]{1,0:T(8,128)(2,1)} %w2.1, ...), custom_call_target="tpu_custom_call" | custom-call | flops 20000000000 | bytes 30000000 | tf_op jit(solution)/shard_map/pallas_call | solution.py:550
  157.0 12.0 %shard_map.101 = bf16[16,1024,128]{2,1,0:T(8,128)(2,1)} custom-call(bf16[16,1024,128]{2,1,0:T(8,128)(2,1)} %get-tuple-element.10.joined, bf16[65,16,128]{2,1,0:T(8,128)(2,1)} %get-tuple-element.11.above, bf16[65,16,128]{2,1,0:T(8,128)(2,1)} %get-tuple-element.12.below, bf16[768,288]{1,0:T(8,128)(2,1)} %get-tuple-element.13.bands, ...), custom_call_target="tpu_custom_call" | custom-call | flops 10000000000 | bytes 10000000 | tf_op jit(solution)/shard_map/pallas_call | solution.py:601

commit v6 on v5

--- a/solution.py
+++ b/solution.py
@@ -86,17 +86,6 @@
 
     lax.fori_loop(1, PEERS, greet, 0)
 
-    repeat = jnp.where(iota((CAP, TL), 1) % CAP == iota((CAP, TL), 0), 1.0, 0.0).astype(BF16)
-    def table(numbers):
-        return lax.dot_general(numbers.astype(F32).astype(BF16), repeat, TN, preferred_element_type=F32)
-
-    scale_table = table(code_rows[...] >> 16) * 0.0625
-    tile_table = table(tile_rows[...] >> 5) * 32.0 + table(tile_rows[...] & 31)
-    for i in range(PEERS // 8):
-        at = slice(i * 8, i * 8 + 8)
-        scale_rows[at] = scale_table[at].reshape(8, 1, TL)
-        tiles[at] = tile_table[at].reshape(8, 1, TL)
-
     def edges(n, carry):
         at = pl.ds(pl.multiple_of(n * 256, 256), 256)
         for half in range(2):
@@ -254,7 +243,6 @@
         inbox[0, q] = value
 
     make(me, 0, put_own)
-    scale_in[0] = scale_rows[me]
 
     def block_copy(t, p):
         return pltpu.make_async_remote_copy(
@@ -276,11 +264,28 @@
 
         make(p, lax.rem(t, 2), put_tile)
 
-        scale_copy(t, p).start()
         block_copy(t, p).start()
         return carry
 
     lax.fori_loop(1, PEERS, send_step, 0)
+
+    repeat = jnp.where(iota((CAP, TL), 1) % CAP == iota((CAP, TL), 0), 1.0, 0.0).astype(BF16)
+    def table(numbers):
+        return lax.dot_general(numbers.astype(F32).astype(BF16), repeat, TN, preferred_element_type=F32)
+
+    scale_table = table(code_rows[...] >> 16) * 0.0625
+    tile_table = table(tile_rows[...] >> 5) * 32.0 + table(tile_rows[...] & 31)
+    for i in range(PEERS // 8):
+        at = slice(i * 8, i * 8 + 8)
+        scale_rows[at] = scale_table[at].reshape(8, 1, TL)
+        tiles[at] = tile_table[at].reshape(8, 1, TL)
+    scale_in[0] = scale_rows[me]
+
+    def send_scale(t, carry):
+        scale_copy(t, peer_of(t)).start()
+        return carry
+
+    lax.fori_loop(1, PEERS, send_scale, 0)
 
     def pick_body(q, carry):
         j, lane = iota((TL, 256), 0), iota((TL, 256), 1)

time: 169 us -> 169 us (level)
  no operation moved by 1% of the time
where the time goes in v6:
time: 169 us
  Pallas kernels  167 us (99%)
    pallas_call x1, Pallas kernels, local(): pl.pallas_call(join_kernel, out_shape=[jax.ShapeDtypeStruct((C, AR_DEV, T...  155 us
    pallas_call x1, Pallas kernels, local(): pl.pallas_call(uv_kernel, out_shape=jax.ShapeDtypeStruct((C, AR_DEV, TL),...  12 us

profile of v6, /device:TPU:1, one launch (start us, length us, event | category | flops | bytes accessed | tf_op | source)
XLA Modules:
  0.0 168.6 jit_solution(1908666937071947961)
XLA Ops:
  0.0 1.3 fusion.1.code.code_rows
  1.3 155.2 %shard_map.100 = (bf16[16,1024,128]{2,1,0:T(8,128)(2,1)}, bf16[65,16,128]{2,1,0:T(8,128)(2,1)}, bf16[65,16,128]{2,1,0:T(8,128)(2,1)}, bf16[768,288]{1,0:T(8,128)(2,1)}, bf16[4,128,128]{2,1,0:T(8,128)(2,1)}) custom-call(bf16[16,32,2048]{2,1,0:T(8,128)(2,1)} %bitcast.18, bf16[16,144]{1,0:T(8,128)(2,1)} %w1.1, bf16[16,144]{1,0:T(8,128)(2,1)} %w2.1, ...), custom_call_target="tpu_custom_call" | custom-call | flops 20000000000 | bytes 30000000 | tf_op jit(solution)/shard_map/pallas_call | solution.py:555
  156.6 12.0 %shard_map.101 = bf16[16,1024,128]{2,1,0:T(8,128)(2,1)} custom-call(bf16[16,1024,128]{2,1,0:T(8,128)(2,1)} %get-tuple-element.10.joined, bf16[65,16,128]{2,1,0:T(8,128)(2,1)} %get-tuple-element.11.above, bf16[65,16,128]{2,1,0:T(8,128)(2,1)} %get-tuple-element.12.below, bf16[768,288]{1,0:T(8,128)(2,1)} %get-tuple-element.13.bands, ...), custom_call_target="tpu_custom_call" | custom-call | flops 10000000000 | bytes 10000000 | tf_op jit(solution)/shard_map/pallas_call | solution.py:606
